TPU v7x, 512 devices: a whole 4x8x8 slice. The times are simulated.
512 devices in a mesh: src: 4 (over x), gx: 8 (over y_lo, core), gy: 16 (over z, y_hi).
Axes of the slice: x: 4, y: 8 (y_hi: 2, y_lo: 4; y = y_hi * 4 + y_lo), z: 8, core: 2. Of those that a mesh axis runs over, the one named last changes fastest.
Arguments:
- cam_send: bfloat16 [32, 16, 32, 2, 16, 256], P(('src', 'gx'), 'gy'), may hold values from -6 to 6
- lidar_bev: bfloat16 [4, 128, 1024, 256], P('src', 'gx', 'gy'), may hold values from -6 to 6
- tile_active: int32 [4, 32, 256], P('src', 'gx', 'gy'), may hold values 0 or 1
- tile_source: int32 [4, 32, 256], P('src', 'gx', 'gy'), may hold values from 0 to 63, as said below
- conv_weight: bfloat16 [3, 3, 256, 256], replicated, may hold values from -0.125 to 0.125
- head_up: bfloat16 [256, 512], replicated, may hold values from -0.375 to 0.375
- head_out: bfloat16 [512, 128], replicated, may hold values from -0.25 to 0.25
- cotangent: bfloat16 [4, 128, 1024, 128], P('src', 'gx', 'gy'), may hold values from -6 to 6
Outputs:
- head_maps: bfloat16 [4, 128, 1024, 128], P('src', 'gx', 'gy')
- grad_lidar: bfloat16 [4, 128, 1024, 256], P('src', 'gx', 'gy')
- grad_cam: bfloat16 [32, 16, 32, 2, 16, 256], P(('src', 'gx'), 'gy')
- grad_conv: float32 [589824], P(('src', 'gx', 'gy'))
- grad_up: float32 [256, 512], replicated
- grad_out: float32 [512, 128], replicated
Inputs may be any that keep to these rules, and one draw needn't show every extreme that they name: `tile_source`: within the 4 x 16 tiles of one sample that fall on one grid device, the values are distinct and take every value of the range; value // 2 is the camera section (index of src+gx) holding the tile, value % 2 its slot.
All inputs are finite; a program needn't handle non-finite values. No bound on the sum of `tile_active` on one device may be relied on, other than what follows from the above.
Results may differ from a plain program's by a relative error of at most 0.007.
Values may be sent and summed in bfloat16 or wider, within the bound.
A program may use at most 64 MiB of HBM per device.

v0:
```python
import math

import jax
import jax.numpy as jnp
from jax import lax
from jax.sharding import PartitionSpec as P


def with_halo(shard, sides, width):
    for axis, dim in sides:
        devices, length = (lax.axis_size(axis), shard.shape[dim])
        up = [(i, (i + 1) % devices) for i in range(devices - 1)]
        down = [(j, i) for i, j in up]
        last = lax.slice_in_dim(shard, length - width, length, axis=dim)
        leading = lax.slice_in_dim(shard, 0, width, axis=dim)
        before = lax.ppermute(last, axis, up)
        after = lax.ppermute(leading, axis, down)
        shard = jnp.concatenate([before, shard, after], axis=dim)
    return shard


def silu_slope(value):
    sigmoid_value = jax.nn.sigmoid(value)
    return sigmoid_value * (1.0 + value * (1.0 - sigmoid_value))


def conv_taps(padded, weight, cells_x, cells_y):
    channels = weight.shape[2]
    summed = jnp.zeros((cells_x * cells_y, weight.shape[3]), jnp.float32)
    for row_tap in range(3):
        for col_tap in range(3):
            window = padded[row_tap : row_tap + cells_x, col_tap : col_tap + cells_y].reshape(
                cells_x * cells_y, channels
            )
            summed = summed + jnp.dot(
                window, weight[row_tap, col_tap], preferred_element_type=jnp.float32
            )
    return summed


def conv_back(padded, weight, cells_x, cells_y):
    channels = weight.shape[3]
    summed = jnp.zeros((cells_x * cells_y, weight.shape[2]), jnp.float32)
    for row_tap in range(3):
        for col_tap in range(3):
            window = padded[
                2 - row_tap : 2 - row_tap + cells_x, 2 - col_tap : 2 - col_tap + cells_y
            ].reshape(cells_x * cells_y, channels)
            summed = summed + jnp.dot(
                window, weight[row_tap, col_tap].T, preferred_element_type=jnp.float32
            )
    return summed


def tap_grads(padded, grad_pre, cells_x, cells_y):
    channels = padded.shape[-1]
    rows_list = []
    for row_tap in range(3):
        row_items = []
        for col_tap in range(3):
            window = padded[row_tap : row_tap + cells_x, col_tap : col_tap + cells_y].reshape(
                cells_x * cells_y, channels
            )
            row_items.append(jnp.dot(window.T, grad_pre, preferred_element_type=jnp.float32))
        rows_list.append(jnp.stack(row_items))
    return jnp.stack(rows_list)


def per_device(
    cam_send, lidar_bev, tile_active, tile_source, conv_weight, head_up, head_out, cotangent
):
    sources = cam_send.shape[2]
    slot_count = cam_send.shape[3]
    tile_cells = cam_send.shape[4]
    channels = cam_send.shape[5]
    tiles_x = tile_active.shape[1]
    tiles_y = tile_active.shape[2]
    cells_x = lidar_bev.shape[1]
    cells_y = lidar_bev.shape[2]
    tile_side = cells_x // tiles_x
    out_width = cotangent.shape[3]
    n_src = lax.axis_size("src")
    n_gx = lax.axis_size("gx")
    n_gy = lax.axis_size("gy")
    scale = 1.0 / math.sqrt(n_src * n_gx * n_gy * cells_x * cells_y)
    outgoing = cam_send.reshape(sources, slot_count, tile_cells, channels)
    arrived = lax.all_to_all(outgoing, ("src", "gx"), split_axis=0, concat_axis=0, tiled=True)
    arrived = arrived.reshape(sources * slot_count, tile_cells, channels)
    tile_rows = tile_source.reshape(tiles_x * tiles_y)
    cam_tiles = jnp.take(arrived, tile_rows, axis=0)
    camera = (
        cam_tiles.reshape(tiles_x, tiles_y, tile_side, tile_side, channels)
        .transpose(0, 2, 1, 3, 4)
        .reshape(cells_x, cells_y, channels)
    )
    occupied = jnp.broadcast_to(
        tile_active[0].astype(jnp.float32)[:, None, :, None],
        (tiles_x, tile_side, tiles_y, tile_side),
    ).reshape(cells_x, cells_y)
    mask_flat = occupied.reshape(cells_x * cells_y, 1)
    merged = (
        occupied[:, :, None] * (camera.astype(jnp.float32) + lidar_bev[0].astype(jnp.float32))
    ).astype(jnp.bfloat16)
    padded = with_halo(merged, (("gx", 0), ("gy", 1)), 1)
    pre_act = conv_taps(padded, conv_weight, cells_x, cells_y)
    feature = (mask_flat * jax.nn.silu(pre_act)).astype(jnp.bfloat16)
    up_act = jnp.dot(feature, head_up, preferred_element_type=jnp.float32)
    hidden = jax.nn.silu(up_act).astype(jnp.bfloat16)
    head_maps = jnp.dot(hidden, head_out, preferred_element_type=jnp.float32).astype(jnp.bfloat16)
    upstream = cotangent[0].reshape(cells_x * cells_y, out_width)
    out_term = jnp.dot(hidden.T, upstream, preferred_element_type=jnp.float32) * scale
    grad_hidden = (
        jnp.dot(upstream, head_out.T, preferred_element_type=jnp.float32) * silu_slope(up_act)
    ).astype(jnp.bfloat16)
    up_term = jnp.dot(feature.T, grad_hidden, preferred_element_type=jnp.float32) * scale
    grad_feat = jnp.dot(grad_hidden, head_up.T, preferred_element_type=jnp.float32)
    grad_pre = (mask_flat * grad_feat * silu_slope(pre_act)).astype(jnp.bfloat16)
    conv_terms = (tap_grads(padded, grad_pre, cells_x, cells_y) * scale).reshape(-1)
    grad_padded = with_halo(grad_pre.reshape(cells_x, cells_y, channels), (("gx", 0), ("gy", 1)), 1)
    grad_merged = conv_back(grad_padded, conv_weight, cells_x, cells_y)
    grad_in = (mask_flat * grad_merged).astype(jnp.bfloat16)
    grad_tiles = (
        grad_in.reshape(tiles_x, tile_side, tiles_y, tile_side, channels)
        .transpose(0, 2, 1, 3, 4)
        .reshape(tiles_x * tiles_y, tile_cells, channels)
    )
    returning = (
        jnp.zeros((sources * slot_count, tile_cells, channels), jnp.bfloat16)
        .at[tile_rows]
        .set(grad_tiles)
    )
    returning = returning.reshape(sources, slot_count, tile_cells, channels)
    grad_cam = lax.all_to_all(returning, ("src", "gx"), split_axis=0, concat_axis=0, tiled=True)
    grad_cam = grad_cam.reshape(1, 1, sources, slot_count, tile_cells, channels)
    grad_up, grad_out = lax.psum((up_term, out_term), ("src", "gx", "gy"))
    grad_conv = lax.psum_scatter(conv_terms, ("src", "gx", "gy"), scatter_dimension=0, tiled=True)
    return (
        head_maps.reshape(1, cells_x, cells_y, out_width),
        grad_in.reshape(1, cells_x, cells_y, channels),
        grad_cam,
        grad_conv,
        grad_up,
        grad_out,
    )


def solution(mesh):
    in_specs = (
        P(("src", "gx"), "gy", None, None, None, None),
        P("src", "gx", "gy", None),
        P("src", "gx", "gy"),
        P("src", "gx", "gy"),
        P(),
        P(),
        P(),
        P("src", "gx", "gy", None),
    )
    out_specs = (
        P("src", "gx", "gy", None),
        P("src", "gx", "gy", None),
        P(("src", "gx"), "gy", None, None, None, None),
        P(("src", "gx", "gy")),
        P(),
        P(),
    )
    return jax.shard_map(
        per_device, mesh=mesh, in_specs=in_specs, out_specs=out_specs, check_vma=False
    )
```

profile of v0, /device:TPU:1, one launch (start us, length us, event | category | flops | bytes accessed | tf_op | source)
XLA Modules:
  0.0 376.6 jit_solution(16057770451095140757)
XLA Ops:
  7.2 10.6 %all-to-all-start = ((bf16[32,2,16,256]{3,2,1,0:T(8,128)(2,1)}), bf16[32,2,16,256]{3,2,1,0:T(8,128)(2,1)S(1)}, u32[]{:S(2)}, u32[]{:S(2)}) async-start(bf16[32,2,16,256]{3,2,1,0:T(8,128)(2,1)} %bitcast.214), calls=%async_computation | async-start | bytes 1048576 | tf_op jit(solution)/shard_map/all_to_all | solution.py:87
  17.8 0.7 convert_bitcast_fusion.1
  19.2 15.5 %all-to-all-done = bf16[32,2,16,256]{3,2,1,0:T(8,128)(2,1)S(1)} async-done(((bf16[32,2,16,256]{3,2,1,0:T(8,128)(2,1)}), bf16[32,2,16,256]{3,2,1,0:T(8,128)(2,1)S(1)}, u32[]{:S(2)}, u32[]{:S(2)}) %all-to-all-start) | async-done | bytes 524320 | tf_op jit(solution)/shard_map/all_to_all | solution.py:87
  34.7 0.6 gather_fusion
  35.6 0.7 copy.24
  36.3 1.3 reshape.203
  37.7 1.3 reshape.206
  39.0 1.5 fusion.9
  40.5 1.9 collective-permute-start
  42.5 2.4 collective-permute-start.1
  44.9 1.0 fusion.7
  45.9 0.4 fusion.11
  46.3 0.4 copy.26
  46.9 0.8 collective-permute-done.1
  47.7 3.2 collective-permute-start.2
  51.0 1.5 collective-permute-start.3
  52.5 0.3 fusion.30
  52.8 6.5 %collective-permute-done.3 = bf16[18,1,256]{2,1,0:T(2,128)(2,1)S(1)} collective-permute-done((bf16[18,1,256]{2,1,0:T(2,128)(2,1)S(1)}, bf16[18,1,256]{2,1,0:T(2,128)(2,1)S(1)}, u32[]{:S(2)}, u32[]{:S(2)}) %collective-permute-start.3) | collective-permute-done | bytes 9248 | tf_op jit(solution)/shard_map/ppermute | solution.py:17
  59.4 0.4 maximum_maximum_fusion
  59.8 0.4 fusion.56
  60.5 0.3 convolution_add_fusion.13
  61.1 0.3 convolution_add_fusion.11
  61.7 0.3 convolution_add_fusion.9
  62.3 0.3 fusion.2
  62.6 0.9 multiply_convert_fusion.1
  63.6 0.9 multiply_convert_fusion
  64.5 0.6 fusion.4
  65.0 0.3 convolution_bitcast_fusion.7
  65.4 0.3 convolution_bitcast_fusion.6
  65.7 0.3 convolution_bitcast_fusion.8
  66.1 0.3 convolution_bitcast_fusion.3
  66.4 0.3 convolution_bitcast_fusion.5
  66.8 0.3 convolution_bitcast_fusion.1
  67.1 0.3 convolution_bitcast_fusion
  67.4 0.3 convolution_bitcast_fusion.2
  67.8 1.6 convolution_multiply_fusion.1
  69.4 0.3 convolution_bitcast_fusion.4
  69.7 1.2 convolution_multiply_fusion.2
  70.9 3.9 %collective-permute-start.4 = (bf16[1,64,256]{2,1,0:T(8,128)(2,1)S(1)}, bf16[1,64,256]{2,1,0:T(8,128)(2,1)S(1)}, u32[]{:S(2)}, u32[]{:S(2)}) collective-permute-start(bf16[1,64,256]{2,1,0:T(8,128)(2,1)S(1)} %get-tuple-element.31), channel_id=1, source_target_pairs={{0,16},{16,32},{32,48},{48,64},{64,80},{80,96},{96,112},{1,17},{17... | collective-permute-start | bytes 98312 | tf_op jit(solution)/shard_map/ppermute | solution.py:16
  74.8 1.9 collective-permute-start.5
  77.2 2.6 copy.30
  80.1 1.3 collective-permute-start.6
  81.4 8.1 %collective-permute-start.7 = (bf16[18,1,256]{2,1,0:T(2,128)(2,1)S(1)}, bf16[18,1,256]{2,1,0:T(2,128)(2,1)S(1)}, u32[]{:S(2)}, u32[]{:S(2)}) collective-permute-start(bf16[18,1,256]{2,1,0:T(2,128)(2,1)S(1)} %get-tuple-element.24), channel_id=1, source_target_pairs={{0,1},{1,2},{2,3},{3,4},{4,5},{5,6},{6,7},{7,8},{8,9},{9,10},{10,1... | collective-permute-start | bytes 27656 | tf_op jit(solution)/shard_map/ppermute | solution.py:16
  89.6 0.3 fusion.28
  90.2 0.4 pad_maximum_fusion.1
  90.6 0.3 fusion.54
  91.1 0.3 convolution_add_fusion.6
  91.4 0.3 convolution_add_fusion.5
  91.7 0.3 convolution_add_fusion.4
  92.1 0.3 convolution_add_fusion.3
  92.4 0.3 convolution_add_fusion.2
  92.7 0.3 convolution_add_fusion.1
  93.1 0.3 fusion.12
  93.4 0.3 fusion.5
  94.5 0.8 broadcast_in_dim.23
  95.4 7.2 %scatter_fusion = bf16[64,16,256]{2,1,0:T(8,128)(2,1)} fusion(bf16[64,16,256]{2,1,0:T(8,128)(2,1)} %broadcast_in_dim.23, s32[64]{0:T(128)S(1)} %fusion.52, bf16[64,16,256]{2,1,0:T(8,128)(2,1)S(1)} %copy.28), kind=kCustom, calls=%fused_computation.1 | custom fusion | bytes 1573120 | tf_op jit(solution)/shard_map/scatter | solution.py:130
  102.5 6.3 %all-to-all-start.1 = ((bf16[32,2,16,256]{3,2,1,0:T(8,128)(2,1)}), bf16[32,2,16,256]{3,2,1,0:T(8,128)(2,1)S(1)}, u32[]{:S(2)}, u32[]{:S(2)}) async-start(bf16[32,2,16,256]{3,2,1,0:T(8,128)(2,1)} %bitcast.41), calls=%async_computation.1 | async-start | bytes 1048576 | tf_op jit(solution)/shard_map/all_to_all | solution.py:133
  108.9 1.1 convolution_convert_fusion
  110.0 17.2 %all-to-all-done.1 = bf16[32,2,16,256]{3,2,1,0:T(8,128)(2,1)S(1)} async-done(((bf16[32,2,16,256]{3,2,1,0:T(8,128)(2,1)}), bf16[32,2,16,256]{3,2,1,0:T(8,128)(2,1)S(1)}, u32[]{:S(2)}, u32[]{:S(2)}) %all-to-all-start.1) | async-done | bytes 524320 | tf_op jit(solution)/shard_map/all_to_all | solution.py:133
  127.2 238.8 %all-reduce.4.cloned.1.call-done = (f32[589824]{0:T(1024)}, f32[256,512]{1,0:T(8,128)}, f32[512,128]{1,0:T(8,128)}) async-done(((f32[589824]{0:T(1024)}, f32[256,512]{1,0:T(8,128)}, f32[512,128]{1,0:T(8,128)}), (f32[589824]{0:T(1024)}, f32[256,512]{1,0:T(8,128)}, f32[512,128]{1,0:T(8,128)})) %all-reduce.4.cloned.1.call-update) | async-done | bytes 3145744
  366.0 1.5 dynamic-slice
  367.5 0.8 copy.41
  368.3 0.8 copy.42
  369.1 0.7 copy.43
  (59 shorter events, 4.4 us)
Async XLA Ops:
  7.2 55.5 %copy-start = (bf16[256,512]{1,0:T(8,128)(2,1)S(1)}, bf16[256,512]{1,0:T(8,128)(2,1)}, u32[]{:S(2)}) copy-start(bf16[256,512]{1,0:T(8,128)(2,1)} %param.13) | copy-start | bytes 786436
  7.2 11.6 %copy-start.10 = (s32[1,4,16]{2,1,0:T(4,128)S(1)}, s32[1,4,16]{2,1,0:T(4,128)}, u32[]{:S(2)}) copy-start(s32[1,4,16]{2,1,0:T(4,128)} %param.11) | copy-start | bytes 772
  7.2 11.7 %copy-start.1 = (bf16[1,16,64,256]{3,2,1,0:T(8,128)(2,1)S(1)}, bf16[1,16,64,256]{3,2,1,0:T(8,128)(2,1)}, u32[]{:S(2)}) copy-start(bf16[1,16,64,256]{3,2,1,0:T(8,128)(2,1)} %param.9) | copy-start | bytes 1572868
  7.2 27.5 %all-to-all-start = ((bf16[32,2,16,256]{3,2,1,0:T(8,128)(2,1)}), bf16[32,2,16,256]{3,2,1,0:T(8,128)(2,1)S(1)}, u32[]{:S(2)}, u32[]{:S(2)}) async-start(bf16[32,2,16,256]{3,2,1,0:T(8,128)(2,1)} %bitcast.214), calls=%async_computation | async-start | bytes 1048576 | tf_op jit(solution)/shard_map/all_to_all | solution.py:87
  17.8 348.2 %all-reduce.4.cloned.1.call-start = ((), (), s32[]{:S(2)}) async-start(), calls=%async_computation.2 | async-start | bytes 6291456
  39.0 5.9 %copy-start.3 = (f32[1024,256]{1,0:T(8,128)S(1)}, f32[1024,256]{1,0:T(8,128)}, u32[]{:S(2)}) copy-start(f32[1024,256]{1,0:T(8,128)} %reshape.206) | copy-start | bytes 3145732
  40.5 6.3 %collective-permute-start = (bf16[1,64,256]{2,1,0:T(8,128)(2,1)S(1)}, bf16[1,64,256]{2,1,0:T(8,128)(2,1)S(1)}, u32[]{:S(2)}, u32[]{:S(2)}) collective-permute-start(bf16[1,64,256]{2,1,0:T(8,128)(2,1)S(1)} %get-tuple-element.35), channel_id=1, source_target_pairs={{0,16},{16,32},{32,48},{48,64},{64,80},{80,96},{96,112},{1,17},{17... | collective-permute-start | bytes 98312 | tf_op jit(solution)/shard_map/ppermute | solution.py:16
  42.5 5.2 %collective-permute-start.1 = (bf16[1,64,256]{2,1,0:T(8,128)(2,1)S(1)}, bf16[1,64,256]{2,1,0:T(8,128)(2,1)S(1)}, u32[]{:S(2)}, u32[]{:S(2)}) collective-permute-start(bf16[1,64,256]{2,1,0:T(8,128)(2,1)S(1)} %get-tuple-element.36), channel_id=1, source_target_pairs={{16,0},{32,16},{48,32},{64,48},{80,64},{96,80},{112,96},{17,1},{33... | collective-permute-start | bytes 98312 | tf_op jit(solution)/shard_map/ppermute | solution.py:17
  46.9 5.7 %copy-start.2 = (bf16[3,3,256,256]{3,2,1,0:T(8,128)(2,1)S(1)}, bf16[3,3,256,256]{3,2,1,0:T(8,128)(2,1)}, u32[]{:S(2)}) copy-start(bf16[3,3,256,256]{3,2,1,0:T(8,128)(2,1)} %param.12) | copy-start | bytes 3538948
  47.7 5.1 %collective-permute-start.2 = (bf16[18,1,256]{2,1,0:T(2,128)(2,1)S(1)}, bf16[18,1,256]{2,1,0:T(2,128)(2,1)S(1)}, u32[]{:S(2)}, u32[]{:S(2)}) collective-permute-start(bf16[18,1,256]{2,1,0:T(2,128)(2,1)S(1)} %get-tuple-element.27), channel_id=1, source_target_pairs={{0,1},{1,2},{2,3},{3,4},{4,5},{5,6},{6,7},{7,8},{8,9},{9,10},{10,1... | collective-permute-start | bytes 27656 | tf_op jit(solution)/shard_map/ppermute | solution.py:16
  51.0 8.4 %collective-permute-start.3 = (bf16[18,1,256]{2,1,0:T(2,128)(2,1)S(1)}, bf16[18,1,256]{2,1,0:T(2,128)(2,1)S(1)}, u32[]{:S(2)}, u32[]{:S(2)}) collective-permute-start(bf16[18,1,256]{2,1,0:T(2,128)(2,1)S(1)} %get-tuple-element.28), channel_id=1, source_target_pairs={{1,0},{2,1},{3,2},{4,3},{5,4},{6,5},{7,6},{8,7},{9,8},{10,9},{11,1... | collective-permute-start | bytes 27656 | tf_op jit(solution)/shard_map/ppermute | solution.py:17
  62.6 1.0 copy-start.8
  62.6 1.0 copy-start.9
  67.8 1.6 copy-start.5
  70.9 8.9 %collective-permute-start.4 = (bf16[1,64,256]{2,1,0:T(8,128)(2,1)S(1)}, bf16[1,64,256]{2,1,0:T(8,128)(2,1)S(1)}, u32[]{:S(2)}, u32[]{:S(2)}) collective-permute-start(bf16[1,64,256]{2,1,0:T(8,128)(2,1)S(1)} %get-tuple-element.31), channel_id=1, source_target_pairs={{0,16},{16,32},{32,48},{48,64},{64,80},{80,96},{96,112},{1,17},{17... | collective-permute-start | bytes 98312 | tf_op jit(solution)/shard_map/ppermute | solution.py:16
  74.8 5.2 %collective-permute-start.5 = (bf16[1,64,256]{2,1,0:T(8,128)(2,1)S(1)}, bf16[1,64,256]{2,1,0:T(8,128)(2,1)S(1)}, u32[]{:S(2)}, u32[]{:S(2)}) collective-permute-start(bf16[1,64,256]{2,1,0:T(8,128)(2,1)S(1)} %get-tuple-element.32), channel_id=1, source_target_pairs={{16,0},{32,16},{48,32},{64,48},{80,64},{96,80},{112,96},{17,1},{33... | collective-permute-start | bytes 98312 | tf_op jit(solution)/shard_map/ppermute | solution.py:17
  80.1 9.8 %collective-permute-start.6 = (bf16[18,1,256]{2,1,0:T(2,128)(2,1)S(1)}, bf16[18,1,256]{2,1,0:T(2,128)(2,1)S(1)}, u32[]{:S(2)}, u32[]{:S(2)}) collective-permute-start(bf16[18,1,256]{2,1,0:T(2,128)(2,1)S(1)} %get-tuple-element.23), channel_id=1, source_target_pairs={{1,0},{2,1},{3,2},{4,3},{5,4},{6,5},{7,6},{8,7},{9,8},{10,9},{11,1... | collective-permute-start | bytes 27656 | tf_op jit(solution)/shard_map/ppermute | solution.py:17
  81.4 8.8 %collective-permute-start.7 = (bf16[18,1,256]{2,1,0:T(2,128)(2,1)S(1)}, bf16[18,1,256]{2,1,0:T(2,128)(2,1)S(1)}, u32[]{:S(2)}, u32[]{:S(2)}) collective-permute-start(bf16[18,1,256]{2,1,0:T(2,128)(2,1)S(1)} %get-tuple-element.24), channel_id=1, source_target_pairs={{0,1},{1,2},{2,3},{3,4},{4,5},{5,6},{6,7},{7,8},{8,9},{9,10},{10,1... | collective-permute-start | bytes 27656 | tf_op jit(solution)/shard_map/ppermute | solution.py:16
  93.8 0.8 copy-start.4
  102.5 24.6 %all-to-all-start.1 = ((bf16[32,2,16,256]{3,2,1,0:T(8,128)(2,1)}), bf16[32,2,16,256]{3,2,1,0:T(8,128)(2,1)S(1)}, u32[]{:S(2)}, u32[]{:S(2)}) async-start(bf16[32,2,16,256]{3,2,1,0:T(8,128)(2,1)} %bitcast.41), calls=%async_computation.1 | async-start | bytes 1048576 | tf_op jit(solution)/shard_map/all_to_all | solution.py:133
  366.0 2.3 copy-start.6
  366.0 3.0 copy-start.7
Sparse Core Ops, SparseCore 0:
  80.0 285.9 all-reduce.3
where the time goes:
time: 378 us; the launch traced here: 377 us
  waiting for transfers between devices  279 us (74%)
  starting transfers between devices  41.2 us (11%)
  local copies, waits for them, and re-layouts  21.4 us (6%)
  matrix products  14.9 us (4%)
  between operations  14.6 us (4%)
  other arithmetic  5.18 us (1%)
    unnamed x2, waiting for transfers between devices  239 us
    all_to_all x1, waiting for transfers between devices, per_device(): lax.all_to_all(returning, ('src', 'gx'), split_axis=0, concat_axis=0, til...  17.2 us
    ppermute x4, starting transfers between devices, with_halo(): before = lax.ppermute(last, axis, up)  17.2 us
    all_to_all x1, waiting for transfers between devices, per_device(): lax.all_to_all(outgoing, ('src', 'gx'), split_axis=0, concat_axis=0, tile...  15.5 us
    all_to_all x1, starting transfers between devices, per_device(): lax.all_to_all(outgoing, ('src', 'gx'), split_axis=0, concat_axis=0, tile...  10.6 us
    ppermute x4, waiting for transfers between devices, with_halo(): after = lax.ppermute(leading, axis, down)  7.57 us
  transfers between devices with their start and end apart: 11, of which 7 were waited for; matrix products, arithmetic and copies ran while one was open for 5% of the time, Pallas kernels for 0%

commit v1 on v0

v1 whole, which is shorter than its diff:
```python
import functools
import math

import jax
import jax.numpy as jnp
from jax import lax
from jax.experimental import pallas as pl
from jax.experimental.pallas import tpu as pltpu
from jax.sharding import PartitionSpec as P

MESH = pl.DeviceIdType.MESH
F32 = jnp.float32
BF16 = jnp.bfloat16


def pad16(rows):
    return (rows + 15) // 16 * 16


def sigmoid(value):
    return 0.5 * jnp.tanh(0.5 * value) + 0.5


def dot(lhs, rhs):
    return jnp.dot(lhs, rhs, preferred_element_type=F32)


def dot_tn(lhs, rhs):
    return lax.dot_general(lhs, rhs, (((0,), (0,)), ((), ())), preferred_element_type=F32)


def rcopy(src, dst, send_sem, recv_sem, device):
    return pltpu.make_async_remote_copy(
        src_ref=src,
        dst_ref=dst,
        send_sem=send_sem,
        recv_sem=recv_sem,
        device_id=device,
        device_id_type=MESH,
    )


class Dims:
    def __init__(self, n_src, n_gx, n_gy, cells_x, cells_y, channels, head, outc):
        self.X, self.GX, self.GY = n_src, n_gx, n_gy
        self.YL, self.Z, self.Y = n_gx // 2, n_gy // 2, n_gx
        self.N = n_src * n_gx
        self.cx, self.cy, self.c = cells_x, cells_y, channels
        self.cells = cells_x * cells_y
        self.tx, self.ty = cells_x // 4, cells_y // 4
        self.tiles = self.tx * self.ty
        self.head, self.outc = head, outc
        self.colp = pad16(cells_x)
        self.rows = 9 * channels
        self.rc = self.rows // 2
        self.rz = self.rc // self.Z
        self.rx = self.rz // self.X
        self.rxp = pad16(self.rx)
        self.hb = 2 * self.rx // self.Y
        self.hbp = pad16(self.hb)
        self.hrows = (channels * head + head * outc) // channels
        self.hc = self.hrows // 2
        self.hx = self.hc // self.X
        self.hz = self.hx // self.Z
        self.hzp = pad16(self.hz)
        self.scale = 1.0 / math.sqrt(n_src * n_gx * n_gy * cells_x * cells_y)


def kernel(
    d,
    cam, lidar_h, act, tsrc, inv, wconv_h, hup_h, hout_h, cot_h,
    maps_o, gin_o, gcam_o, gconv_o, gup_o, gout_o,
    arrived, lidar, wconv, hup, hout, cot,
    wt, hup_t, hout_t, mask,
    m32, m3, g3, rows_s, rows_r, cols_s, cols_r,
    feat, hid, gh, maps, gp, gi, tiles, ret,
    dw32, dwb, core_r, cs32, zs, z_r, zsum, xs32, xsb, x_r, hrow, ls, l_r,
    h32, hb, hcore_r, hs32, hxs, hx_r, hxsum, hzs32, hzs, hz_r, hy, hy_r, hall,
    in_sem, out_sem,
    a_send, a_recv, b_send, b_recv,
    halo_send, halo_recv, core_send, core_recv,
    z_send, z_recv, x_send, x_recv, l_send, l_recv,
    hx_send, hx_recv, hz_send, hz_recv, hy_send, hy_recv,
    gz_send, gz_recv, gx_send, gx_recv,
):
    s = lax.axis_index("src")
    g = lax.axis_index("gx")
    r = lax.axis_index("gy")
    core, yl = g % 2, g // 2
    z, yh = r // 2, r % 2
    me = s * d.GX + g
    X, Y, Z, N, C, CY = d.X, d.Y, d.Z, d.N, d.c, d.cy

    loads = [
        pltpu.make_async_copy(src, dst, in_sem.at[k])
        for k, (src, dst) in enumerate(
            [(lidar_h, lidar), (wconv_h, wconv), (hup_h, hup), (hout_h, hout), (cot_h, cot),
             (cam.at[me], arrived.at[me])]
        )
    ]
    for load in loads:
        load.start()

    def a_peer(step):
        other = (me + step) % N
        return (other // d.GX, other % d.GX, r)

    def z_peer(step):
        return (s, g, ((z + step) % Z) * 2 + yh)

    def x_peer(step):
        return ((s + step) % X, g, r)

    def y_peer(step):
        at = (yl * 2 + yh + step) % Y
        return (s, (at // 2) * 2 + core, z * 2 + at % 2)

    other_core = (s, yl * 2 + 1 - core, r)

    block0 = ((core * Z + z) * X + s) * Y
    my_block = (s * d.GX + g) * d.GY + r
    group = my_block // Y
    from_core, from_z, from_x = group // (Z * X), (group // X) % Z, group % X

    def owner(block):
        at = block0 + block
        return (at // (d.GX * d.GY), (at // d.GY) % d.GX, at % d.GY)

    def last_sender(at):
        return (from_x, (at // 2) * 2 + from_core, from_z * 2 + at % 2)

    self_group = jnp.logical_and(
        jnp.logical_and(from_core == core, from_z == z), from_x == s
    )
    my_y = yl * 2 + yh

    barrier = pltpu.get_barrier_semaphore()

    def greet(device):
        pl.semaphore_signal(barrier, inc=1, device_id=device, device_id_type=MESH)

    def greet_a(step, _):
        greet(a_peer(step))
        return 0

    lax.fori_loop(1, N, greet_a, 0)
    count = N - 1
    for step in range(1, Z):
        greet(z_peer(step))
        count += 1
    for at in range(d.YL):
        greet((s, at * 2 + core, z * 2 + 1 - yh))
        count += 1
    for side in (-1, 1):
        for near in (-1, 0, 1):
            greet((s, (g + near + d.GX) % d.GX, (r + side + d.GY) % d.GY))
            count += 1
    for at in range(Y):
        is_self = jnp.logical_and(self_group, my_y == at)

        @pl.when(jnp.logical_not(is_self))
        def _():
            greet(last_sender(at))

    count = count + Y - jnp.where(self_group, 1, 0)
    pl.semaphore_wait(barrier, count)

    def a_copy(step):
        return rcopy(
            cam.at[(me + step) % N], arrived.at[me], a_send.at[step], a_recv.at[step], a_peer(step)
        )

    def a_start(step, _):
        a_copy(step).start()
        return 0

    lax.fori_loop(1, N, a_start, 0)

    for load in loads[:5]:
        load.wait()
    at_y = lax.broadcasted_iota(jnp.int32, (CY, d.ty), 0) // 4
    at_q = lax.broadcasted_iota(jnp.int32, (CY, d.ty), 1)
    for p in range(d.tx):
        row = act[p : p + 1, :].astype(F32)
        column = jnp.sum(jnp.where(at_y == at_q, row, 0.0), axis=1, keepdims=True)
        mask[p] = jnp.broadcast_to(column, (CY, C))
    for i in range(3):
        for j in range(3):
            tap = wconv[2 - i, (2 - j) * C : (3 - j) * C, :].astype(F32)
            wt[i, j * C : (j + 1) * C, :] = tap.T.astype(BF16)
    hup_t[...] = hup[...].astype(F32).T.astype(BF16)
    hout_t[...] = hout[...].astype(F32).T.astype(BF16)

    def a_wait(step, _):
        sender = (me - step + N) % N
        rcopy(
            cam.at[sender], arrived.at[sender], a_send.at[step], a_recv.at[step], a_peer(step)
        ).wait_recv()
        return 0

    lax.fori_loop(1, N, a_wait, 0)
    loads[5].wait()

    span = 4 * CY

    def merge(p, _):
        for q in range(d.ty):
            at = tsrc[p, q]
            tile = arrived[at // 2, at % 2].astype(F32)
            for dx in range(4):
                m32[4 * p + dx, 4 * q : 4 * q + 4, :] = tile[4 * dx : 4 * dx + 4]
        for dx in range(4):
            x = 4 * p + dx
            line = pl.ds(pl.multiple_of(x * CY, CY), CY)
            m32[x] = mask[p] * (m32[x] + lidar[line, :].astype(F32))
        return 0

    lax.fori_loop(0, d.tx, merge, 0)

    def halo_copies(k):
        copies = []
        for side, step in ((0, -1), (1, 1)):
            copies.append(
                (rows_s.at[k, side], rows_r.at[k, 1 - side], (s, (g + step + d.GX) % d.GX, r))
            )
            for near in (-1, 0, 1):
                device = (s, (g + near + d.GX) % d.GX, (r + step + d.GY) % d.GY)
                copies.append((cols_s.at[k, side], cols_r.at[k, 1 - side, 1 - near], device))
        return [
            rcopy(src, dst, halo_send.at[k, n], halo_recv.at[k, n], device)
            for n, (src, dst, device) in enumerate(copies)
        ]

    def halo_start(k):
        rows_s[k, 0] = m32[0].astype(BF16)
        rows_s[k, 1] = m32[d.cx - 1].astype(BF16)
        cols_s[k, 0, 0 : d.cx, :] = m32[:, 0, :].astype(BF16)
        cols_s[k, 1, 0 : d.cx, :] = m32[:, CY - 1, :].astype(BF16)
        copies = halo_copies(k)
        for copy in copies:
            copy.start()
        return copies

    def halo_finish(k, copies, out3):
        for copy in copies:
            copy.wait_recv()
        at = lax.broadcasted_iota(jnp.int32, (CY, C), 0)
        ok_g = (g > 0, g < d.GX - 1)
        ok_r = (r > 0, r < d.GY - 1)

        def put(x, line, left, right):
            down = jnp.where(at == 0, left, pltpu.roll(line, 1, 0))
            up = jnp.where(at == CY - 1, right, pltpu.roll(line, CY - 1, 0))
            out3[x * CY : (x + 1) * CY, 0:C] = down.astype(BF16)
            out3[x * CY : (x + 1) * CY, C : 2 * C] = line.astype(BF16)
            out3[x * CY : (x + 1) * CY, 2 * C : 3 * C] = up.astype(BF16)

        def column(side, near, x, ok):
            value = cols_r[k, side, near].astype(F32)[x : x + 1]
            return jnp.where(ok, value, 0.0)

        for x in range(d.cx):
            left = column(0, 1, x, ok_r[0])
            right = column(1, 1, x, ok_r[1])
            put(x + 1, m32[x], left, right)
        for side, x, row in ((0, 0, d.cx - 1), (1, d.cx + 1, 0)):
            line = jnp.where(ok_g[side], rows_r[k, side].astype(F32), 0.0)
            near = 0 if side == 0 else 2
            left = column(0, near, row, jnp.logical_and(ok_g[side], ok_r[0]))
            right = column(1, near, row, jnp.logical_and(ok_g[side], ok_r[1]))
            put(x, line, left, right)

    halo0 = halo_start(0)
    halo_finish(0, halo0, m3)

    def forward(p, _):
        here = pl.ds(pl.multiple_of(p * span, span), span)
        pre = jnp.zeros((span, C), F32)
        for i in range(3):
            pre = pre + dot(
                m3[pl.ds(pl.multiple_of(p * span + i * CY, CY), span), :], wconv[i]
            )
        occupied = jnp.concatenate([mask[p]] * 4, axis=0)
        sig = sigmoid(pre)
        feature = (occupied * (pre * sig)).astype(BF16)
        slope = occupied * (sig * (1.0 + pre * (1.0 - sig)))
        feat[here, :] = feature
        lines = pl.ds(4 * p, 4)
        m32[lines] = slope.reshape(4, CY, C)
        up = dot(feature, hup[...])
        sig = sigmoid(up)
        hidden = (up * sig).astype(BF16)
        hid[here, :] = hidden
        maps[here, :] = dot(hidden, hout[...]).astype(BF16)
        grad = (dot(cot[here, :], hout_t[...]) * (sig * (1.0 + up * (1.0 - sig)))).astype(BF16)
        gh[here, :] = grad
        value = dot(grad, hup_t[...]) * m32[lines].reshape(span, C)
        m32[lines] = value.reshape(4, CY, C)
        gp[here, :] = value.astype(BF16)
        return 0

    lax.fori_loop(0, d.tx, forward, 0)
    halo1 = halo_start(1)
    maps_out = pltpu.make_async_copy(maps, maps_o, out_sem.at[0])
    maps_out.start()

    def tap_grads(i, _):
        for j in range(3):
            term = dot_tn(
                m3[pl.ds(pl.multiple_of(i * CY, CY), d.cells), j * C : (j + 1) * C], gp[...]
            )
            at = pl.ds(pl.multiple_of(i * (3 * C) + j * C, C), C)
            dw32[at, :] = term
            dwb[at, :] = term.astype(BF16)
        return 0

    lax.fori_loop(0, 3, tap_grads, 0)
    mine = pl.ds(pl.multiple_of(core * d.rc, d.rc), d.rc)
    theirs = pl.ds(pl.multiple_of((1 - core) * d.rc, d.rc), d.rc)
    core_copy = rcopy(dwb.at[theirs], core_r, core_send.at[0], core_recv.at[0], other_core)
    core_copy.start()

    term = dot_tn(feat[...], gh[...])
    for half in range(d.head // C):
        h32[half * C : (half + 1) * C, :] = term[:, half * C : (half + 1) * C]
    base = d.head
    term = dot_tn(hid[...], cot[...])
    depth = d.head // 2
    for half in range(2):
        h32[base : base + depth, half * d.outc : (half + 1) * d.outc] = term[
            half * depth : (half + 1) * depth, :
        ]
    hb[...] = h32[...].astype(BF16)
    hmine = pl.ds(pl.multiple_of(core * d.hc, d.hc), d.hc)
    htheirs = pl.ds(pl.multiple_of((1 - core) * d.hc, d.hc), d.hc)
    hcore_copy = rcopy(hb.at[htheirs], hcore_r, core_send.at[1], core_recv.at[1], other_core)
    hcore_copy.start()

    core_copy.wait_recv()
    cs32[...] = dw32[mine, :] + core_r[...].astype(F32)
    for k in range(Z):
        zs[k] = cs32[k * d.rz : (k + 1) * d.rz, :].astype(BF16)
    z_copies = [
        rcopy(zs.at[(z + k) % Z], z_r.at[k - 1], z_send.at[k], z_recv.at[k], z_peer(k))
        for k in range(1, Z)
    ]
    for copy in z_copies:
        copy.start()

    hcore_copy.wait_recv()
    hs32[...] = h32[hmine, :] + hcore_r[...].astype(F32)
    for k in range(X):
        hxs[k] = hs32[k * d.hx : (k + 1) * d.hx, :].astype(BF16)
    hx_copies = [
        rcopy(hxs.at[(s + k) % X], hx_r.at[k - 1], hx_send.at[k], hx_recv.at[k], x_peer(k))
        for k in range(1, X)
    ]
    for copy in hx_copies:
        copy.start()

    halo_finish(1, halo1, g3)

    def backward(p, _):
        here = pl.ds(pl.multiple_of(p * span, span), span)
        acc = jnp.zeros((span, C), F32)
        for i in range(3):
            acc = acc + dot(g3[pl.ds(pl.multiple_of(p * span + i * CY, CY), span), :], wt[i])
        acc = acc * jnp.concatenate([mask[p]] * 4, axis=0)
        gi[here, :] = acc.astype(BF16)
        m32[pl.ds(4 * p, 4)] = acc.reshape(4, CY, C)
        for q in range(d.ty):
            parts = [m32[4 * p + dx, 4 * q : 4 * q + 4, :] for dx in range(4)]
            tiles[p * d.ty + q] = jnp.concatenate(parts, axis=0).astype(BF16)
        return 0

    lax.fori_loop(0, d.tx, backward, 0)
    gin_out = pltpu.make_async_copy(gi, gin_o, out_sem.at[1])
    gin_out.start()

    def b_copy(step):
        other = (me + step) % N
        return rcopy(
            ret.at[other], gcam_o.at[me], b_send.at[step], b_recv.at[step], a_peer(step)
        )

    def fill(other, _):
        for slot in range(2):
            ret[other, slot] = tiles[inv[other * 2 + slot]]
        return 0

    lax.fori_loop(0, N, fill, 0)

    def b_start(step, _):
        b_copy(step).start()
        return 0

    lax.fori_loop(1, N, b_start, 0)
    own_out = pltpu.make_async_copy(ret.at[me], gcam_o.at[me], out_sem.at[2])
    own_out.start()

    for copy in hx_copies:
        copy.wait_recv()
    total = hs32[pl.ds(pl.multiple_of(s * d.hx, d.hx), d.hx), :]
    for k in range(X - 1):
        total = total + hx_r[k].astype(F32)
    hxsum[0 : d.hx, :] = total
    for k in range(Z):
        part = hxsum[k * d.hz : k * d.hz + d.hzp, :]
        hzs32[k] = part
        hzs[k] = part.astype(BF16)
    hz_copies = [
        rcopy(hzs.at[(z + k) % Z], hz_r.at[k - 1], hz_send.at[k], hz_recv.at[k], z_peer(k))
        for k in range(1, Z)
    ]
    for copy in hz_copies:
        copy.start()
    for copy in hz_copies:
        copy.wait_recv()
    total = hzs32[z]
    for k in range(Z - 1):
        total = total + hz_r[k].astype(F32)
    hy[...] = total.astype(BF16)
    hy_copies = [
        rcopy(hy, hy_r.at[k - 1], hy_send.at[k], hy_recv.at[k], y_peer(k)) for k in range(1, Y)
    ]
    for copy in hy_copies:
        copy.start()
    for copy in hy_copies:
        copy.wait_recv()
    total = hy[...].astype(F32)
    for k in range(Y - 1):
        total = total + hy_r[k].astype(F32)
    hall[core, s, z] = total.astype(BF16)
    gz_copies = [
        rcopy(hall.at[core, s, z], hall.at[core, s, z], gz_send.at[k], gz_recv.at[k], z_peer(k))
        for k in range(1, Z)
    ]
    for copy in gz_copies:
        copy.start()

    for copy in z_copies:
        copy.wait_recv()
    total = cs32[pl.ds(pl.multiple_of(z * d.rz, d.rz), d.rz), :]
    for k in range(Z - 1):
        total = total + z_r[k].astype(F32)
    zsum[0 : d.rz, :] = total
    for k in range(X):
        part = zsum[k * d.rx : k * d.rx + d.rxp, :]
        xs32[k] = part
        xsb[k] = part.astype(BF16)
    x_copies = [
        rcopy(xsb.at[(s + k) % X], x_r.at[k - 1], x_send.at[k], x_recv.at[k], x_peer(k))
        for k in range(1, X)
    ]
    for copy in x_copies:
        copy.start()

    for k, copy in enumerate(gz_copies):
        sender = (z - k - 1 + Z) % Z
        rcopy(
            hall.at[core, s, sender], hall.at[core, s, sender], gz_send.at[k + 1],
            gz_recv.at[k + 1], z_peer(k + 1),
        ).wait_recv()
    gx_copies = [
        rcopy(hall.at[core, s], hall.at[core, s], gx_send.at[k], gx_recv.at[k], x_peer(k))
        for k in range(1, X)
    ]
    for copy in gx_copies:
        copy.start()

    for copy in x_copies:
        copy.wait_recv()
    total = xs32[s]
    for k in range(X - 1):
        total = total + x_r[k].astype(F32)
    hrow[pl.ds(0, d.rxp, stride=2), :] = total[:, 0:128]
    hrow[pl.ds(1, d.rxp, stride=2), :] = total[:, 128:256]
    for k in range(Y):
        ls[k] = hrow[k * d.hb : k * d.hb + d.hbp, :].astype(BF16)
    for k in range(Y):
        is_self = my_block == block0 + k
        copy = rcopy(ls.at[k], l_r.at[my_y], l_send.at[k], l_recv.at[my_y], owner(k))
        local = pltpu.make_async_copy(ls.at[k], l_r.at[my_y], l_recv.at[my_y])

        @pl.when(jnp.logical_not(is_self))
        def _():
            copy.start()

        @pl.when(is_self)
        def _():
            local.start()

    for k in range(1, X):
        sender = (s - k + X) % X
        rcopy(
            hall.at[core, sender], hall.at[core, sender], gx_send.at[k], gx_recv.at[k], x_peer(k)
        ).wait_recv()
    gcore = rcopy(hall.at[core], hall.at[core], core_send.at[2], core_recv.at[2], other_core)
    gcore.start()

    total = jnp.zeros((d.hbp, 128), F32)
    for k in range(Y):
        pltpu.make_async_copy(ls.at[k], l_r.at[k], l_recv.at[k]).wait()
    for k in range(Y):
        total = total + l_r[k].astype(F32)
    gconv_o[...] = total[0 : d.hb, :] * d.scale

    rcopy(
        hall.at[1 - core], hall.at[1 - core], core_send.at[2], core_recv.at[2], other_core
    ).wait_recv()
    for c in range(2):
        for x in range(X):
            for k in range(Z):
                at = c * d.hc + x * d.hx + k * d.hz
                h32[at : at + d.hz, :] = hall[c, x, k].astype(F32)[0 : d.hz, :]
    for half in range(d.head // C):
        gup_o[:, half * C : (half + 1) * C] = h32[half * C : (half + 1) * C, :] * d.scale
    for half in range(2):
        gout_o[half * depth : (half + 1) * depth, :] = (
            h32[base : base + depth, half * d.outc : (half + 1) * d.outc] * d.scale
        )

    def b_wait(step, _):
        sender = (me - step + N) % N
        rcopy(
            ret.at[sender], gcam_o.at[sender], b_send.at[step], b_recv.at[step], a_peer(step)
        ).wait_recv()
        return 0

    lax.fori_loop(1, N, b_wait, 0)

    def drain(step, _):
        a_copy(step).wait_send()
        b_copy(step).wait_send()
        return 0

    lax.fori_loop(1, N, drain, 0)
    for copy in (
        halo0 + halo1 + z_copies + x_copies + hx_copies + hz_copies + hy_copies
        + gz_copies + gx_copies + [core_copy, hcore_copy, gcore]
    ):
        copy.wait_send()
    for k in range(Y):
        copy = rcopy(ls.at[k], l_r.at[my_y], l_send.at[k], l_recv.at[my_y], owner(k))

        @pl.when(my_block != block0 + k)
        def _():
            copy.wait_send()

    maps_out.wait()
    gin_out.wait()
    own_out.wait()


def per_device(
    cam_send, lidar_bev, tile_active, tile_source, conv_weight, head_up, head_out, cotangent
):
    channels = cam_send.shape[5]
    cells_x, cells_y = lidar_bev.shape[1], lidar_bev.shape[2]
    head, outc = head_out.shape
    d = Dims(
        lax.axis_size("src"), lax.axis_size("gx"), lax.axis_size("gy"),
        cells_x, cells_y, channels, head, outc,
    )
    C, X, Y, Z, N = d.c, d.X, d.Y, d.Z, d.N
    cells = d.cells
    rows = tile_source.reshape(1, d.tiles)
    slots = jnp.arange(d.tiles, dtype=jnp.int32)
    inverse = jnp.sum(jnp.where(rows == slots[:, None], slots[None, :], 0), axis=1)

    vmem = pl.BlockSpec(memory_space=pltpu.VMEM)
    smem = pl.BlockSpec(memory_space=pltpu.SMEM)
    anyw = pl.BlockSpec(memory_space=pl.ANY)
    dma = pltpu.SemaphoreType.DMA

    def b16(*shape):
        return pltpu.VMEM(shape, BF16)

    def f32(*shape):
        return pltpu.VMEM(shape, F32)

    scratch = [
        b16(N, 2, 16, C), b16(cells, C), b16(3, 3 * C, C), b16(C, head), b16(head, outc),
        b16(cells, outc),
        b16(3, 3 * C, C), b16(head, C), b16(outc, head), f32(d.tx, cells_y, C),
        f32(cells_x, cells_y, C), b16((cells_x + 2) * cells_y, 3 * C), b16((cells_x + 2) * cells_y, 3 * C),
        b16(2, 2, cells_y, C), b16(2, 2, cells_y, C),
        b16(2, 2, d.colp, C), b16(2, 2, 3, d.colp, C),
        b16(cells, C), b16(cells, head), b16(cells, head), b16(cells, outc), b16(cells, C),
        b16(cells, C), b16(d.tiles, 16, C), b16(N, 2, 16, C),
        f32(d.rows, C), b16(d.rows, C), b16(d.rc, C), f32(d.rc, C),
        b16(Z, d.rz, C), b16(Z - 1, d.rz, C), f32(d.rz + 16, C),
        f32(X, d.rxp, C), b16(X, d.rxp, C), b16(X - 1, d.rxp, C),
        f32(2 * d.rxp + 16, 128), b16(Y, d.hbp, 128), b16(Y, d.hbp, 128),
        f32(d.hrows, C), b16(d.hrows, C), b16(d.hc, C), f32(d.hc, C),
        b16(X, d.hx, C), b16(X - 1, d.hx, C), f32(d.hx + 16, C),
        f32(Z, d.hzp, C), b16(Z, d.hzp, C), b16(Z - 1, d.hzp, C),
        b16(d.hzp, C), b16(Y - 1, d.hzp, C), b16(2, X, Z, d.hzp, C),
        dma((6,)), dma((3,)),
        dma((N,)), dma((N,)), dma((N,)), dma((N,)),
        dma((2, 8)), dma((2, 8)), dma((3,)), dma((3,)),
        dma((Z,)), dma((Z,)), dma((X,)), dma((X,)), dma((Y,)), dma((Y,)),
        dma((X,)), dma((X,)), dma((Z,)), dma((Z,)), dma((Y,)), dma((Y,)),
        dma((Z,)), dma((Z,)), dma((X,)), dma((X,)),
    ]
    maps, gin, gcam, gconv, gup, gout = pl.pallas_call(
        functools.partial(kernel, d),
        out_shape=(
            jax.ShapeDtypeStruct((cells, outc), BF16),
            jax.ShapeDtypeStruct((cells, C), BF16),
            jax.ShapeDtypeStruct((N, 2, 16, C), BF16),
            jax.ShapeDtypeStruct((d.hb, 128), F32),
            jax.ShapeDtypeStruct((C, head), F32),
            jax.ShapeDtypeStruct((head, outc), F32),
        ),
        in_specs=[anyw, anyw, vmem, smem, smem, anyw, anyw, anyw, anyw],
        out_specs=(anyw, anyw, anyw, vmem, vmem, vmem),
        scratch_shapes=scratch,
        compiler_params=pltpu.CompilerParams(
            collective_id=0, has_side_effects=True, vmem_limit_bytes=48 * 1024 * 1024
        ),
    )(
        cam_send.reshape(N, 2, 16, C),
        lidar_bev.reshape(cells, C),
        tile_active.reshape(d.tx, d.ty),
        tile_source.reshape(d.tx, d.ty),
        inverse,
        conv_weight.reshape(3, 3 * C, C),
        head_up,
        head_out,
        cotangent.reshape(cells, outc),
    )
    return (
        maps.reshape(1, cells_x, cells_y, outc),
        gin.reshape(1, cells_x, cells_y, C),
        gcam.reshape(1, 1, N, 2, 16, C),
        gconv.reshape(-1),
        gup,
        gout,
    )


def solution(mesh):
    in_specs = (
        P(("src", "gx"), "gy", None, None, None, None),
        P("src", "gx", "gy", None),
        P("src", "gx", "gy"),
        P("src", "gx", "gy"),
        P(),
        P(),
        P(),
        P("src", "gx", "gy", None),
    )
    out_specs = (
        P("src", "gx", "gy", None),
        P("src", "gx", "gy", None),
        P(("src", "gx"), "gy", None, None, None, None),
        P(("src", "gx", "gy")),
        P(),
        P(),
    )
    return jax.shard_map(
        per_device, mesh=mesh, in_specs=in_specs, out_specs=out_specs, check_vma=False
    )
```

time: 378 us -> 99.7 us (0.26)
  waiting for transfers between devices: 279 us -> 0 us
  Pallas kernels: 0 us -> 85.4 us
  starting transfers between devices: 41.2 us -> 0 us
  matrix products: 14.9 us -> 0 us
  between operations: 14.6 us -> 0.66 us
  local copies, waits for them, and re-layouts: 21.4 us -> 12.7 us
  other arithmetic: 5.18 us -> 0.11 us
    unnamed x2 -> x0, waiting for transfers between devices: 239 us -> none
    pallas_call x0 -> x1, Pallas kernels: none -> 85.4 us  [per_device(): pl.pallas_call(functools.partial(kernel, d), out_shape=(jax.ShapeDtypeStr...]
    all_to_all x2 -> x0, waiting for transfers between devices: 32.7 us -> none  [the longest x1 17.2 us: per_device(): lax.all_to_all(returning, ('src', 'gx'), split_axis=0, concat_axis=0, til...]
    ppermute x8 -> x0, starting transfers between devices: 24.3 us -> none  [the longest x4 17.2 us: with_halo(): before = lax.ppermute(last, axis, up)]
    all_to_all x2 -> x0, starting transfers between devices: 16.9 us -> none  [the longest x1 10.6 us: per_device(): lax.all_to_all(outgoing, ('src', 'gx'), split_axis=0, concat_axis=0, tile...]
    dot_general x33 -> x0, matrix products: 14.9 us -> none  [the longest x9 3.04 us: tap_grads(): jnp.dot(window.T, grad_pre, preferred_element_type=jnp.float32)]
    ppermute x8 -> x0, waiting for transfers between devices: 7.81 us -> none  [the longest x4 7.57 us: with_halo(): after = lax.ppermute(leading, axis, down)]
    scatter x1 -> x0, local copies, waits for them, and re-layouts: 7.16 us -> none  [per_device(): returning = jnp.zeros((sources * slot_count, tile_cells, channels), jnp.b...]
  transfers between devices with their start and end apart: 11 -> 0, of which waited for: 7 -> 0; matrix products, arithmetic and copies ran while one was open for 5% -> 0% of each run, Pallas kernels for 0% -> 0%
where the time goes in v1:
time: 99.7 us; the launch traced here: 98.9 us
  Pallas kernels  85.4 us (86%)
  local copies, waits for them, and re-layouts  12.7 us (13%)
    pallas_call x1, Pallas kernels, per_device(): pl.pallas_call(functools.partial(kernel, d), out_shape=(jax.ShapeDtypeStr...  85.4 us
    unnamed x22, local copies, waits for them, and re-layouts  11.9 us

profile of v1, /device:TPU:1, one launch (start us, length us, event | category | flops | bytes accessed | tf_op | source)
XLA Modules:
  0.0 98.9 jit_solution(9587491937035952575)
XLA Ops:
  0.6 0.8 eq.15
  1.4 0.1 select_reduce_fusion.inv
  1.5 0.0 copy-start
  1.5 1.3 %copy-done = bf16[3,3,256,256]{3,2,1,0:T(8,128)(2,1)S(1)} copy-done((bf16[3,3,256,256]{3,2,1,0:T(8,128)(2,1)S(1)}, bf16[3,3,256,256]{3,2,1,0:T(8,128)(2,1)}, u32[]{:S(2)}) %copy-start) | copy-done | bytes 1179672
  2.8 0.0 copy-start.1
  2.8 1.0 %copy-done.1 = bf16[1,1,32,2,16,256]{5,4,3,2,1,0:T(8,128)(2,1)S(1)} copy-done((bf16[1,1,32,2,16,256]{5,4,3,2,1,0:T(8,128)(2,1)S(1)}, bf16[1,1,32,2,16,256]{5,4,3,2,1,0:T(8,128)(2,1)}, u32[]{:S(2)}) %copy-start.1) | copy-done | bytes 524312
  3.8 0.0 copy-start.2
  3.8 1.0 %copy-done.2 = bf16[1,16,64,256]{3,2,1,0:T(8,128)(2,1)S(1)} copy-done((bf16[1,16,64,256]{3,2,1,0:T(8,128)(2,1)S(1)}, bf16[1,16,64,256]{3,2,1,0:T(8,128)(2,1)}, u32[]{:S(2)}) %copy-start.2) | copy-done | bytes 524312
  4.9 0.0 copy-start.3
  4.9 0.9 copy-done.3
  5.8 0.0 copy-start.4
  5.8 0.9 copy-done.4
  6.8 0.0 copy-start.5
  6.8 0.9 copy-done.5
  7.7 0.0 copy-start.6
  7.7 0.7 copy-done.6
  8.4 0.0 copy-start.7
  8.4 0.7 copy-done.7
  9.0 85.4 %shard_map.127 = (bf16[1024,128]{1,0:T(8,128)(2,1)S(1)}, bf16[1024,256]{1,0:T(8,128)(2,1)S(1)}, bf16[32,2,16,256]{3,2,1,0:T(8,128)(2,1)S(1)}, f32[9,128]{1,0:T(8...) custom-call(bf16[32,2,16,256]{3,2,1,0:T(8,128)(2,1)S(1)} %bitcast.11, bf16[1024,256]{1,0:T(8,128)(2,1)S(1)} %bitcast.12, ...), custom_call_target="tpu_custom_call" | custom-call | tf_op jit(solution)/shard_map/pallas_call | solution.py:606
  94.5 0.7 copy.20
  95.2 0.8 copy.21
  96.0 0.8 copy.22
  96.8 0.6 copy.23
  97.4 0.8 copy.24
  98.2 0.7 copy.25
Async XLA Ops:
  1.5 1.3 %copy-start = (bf16[3,3,256,256]{3,2,1,0:T(8,128)(2,1)S(1)}, bf16[3,3,256,256]{3,2,1,0:T(8,128)(2,1)}, u32[]{:S(2)}) copy-start(bf16[3,3,256,256]{3,2,1,0:T(8,128)(2,1)} %param.12) | copy-start | bytes 3538948
  2.8 1.0 %copy-start.1 = (bf16[1,1,32,2,16,256]{5,4,3,2,1,0:T(8,128)(2,1)S(1)}, bf16[1,1,32,2,16,256]{5,4,3,2,1,0:T(8,128)(2,1)}, u32[]{:S(2)}) copy-start(bf16[1,1,32,2,16,256]{5,4,3,2,1,0:T(8,128)(2,1)} %param.8) | copy-start | bytes 1572868
  3.8 1.0 %copy-start.2 = (bf16[1,16,64,256]{3,2,1,0:T(8,128)(2,1)S(1)}, bf16[1,16,64,256]{3,2,1,0:T(8,128)(2,1)}, u32[]{:S(2)}) copy-start(bf16[1,16,64,256]{3,2,1,0:T(8,128)(2,1)} %param.9) | copy-start | bytes 1572868
  4.9 0.9 copy-start.3
  5.8 0.9 copy-start.4
  6.8 0.9 copy-start.5
  7.7 0.7 copy-start.6
  8.4 0.7 copy-start.7

commit v2 on v1

v2 whole, which is shorter than its diff:
```python
import functools
import math

import jax
import jax.numpy as jnp
from jax import lax
from jax.experimental import pallas as pl
from jax.experimental.pallas import tpu as pltpu
from jax.sharding import PartitionSpec as P

MESH = pl.DeviceIdType.MESH
F32 = jnp.float32
BF16 = jnp.bfloat16


def pad16(rows):
    return (rows + 15) // 16 * 16


def sigmoid(value):
    return 0.5 * jnp.tanh(0.5 * value) + 0.5


def dot(lhs, rhs):
    return jnp.dot(lhs, rhs, preferred_element_type=F32)


def dot_tn(lhs, rhs):
    return lax.dot_general(lhs, rhs, (((0,), (0,)), ((), ())), preferred_element_type=F32)


def rcopy(src, dst, send_sem, recv_sem, device):
    return pltpu.make_async_remote_copy(
        src_ref=src,
        dst_ref=dst,
        send_sem=send_sem,
        recv_sem=recv_sem,
        device_id=device,
        device_id_type=MESH,
    )


class Dims:
    def __init__(self, n_src, n_gx, n_gy, cells_x, cells_y, channels, head, outc):
        self.X, self.GX, self.GY = n_src, n_gx, n_gy
        self.YL, self.Z, self.Y = n_gx // 2, n_gy // 2, n_gx
        self.N = n_src * n_gx
        self.cx, self.cy, self.c = cells_x, cells_y, channels
        self.cells = cells_x * cells_y
        self.tx, self.ty = cells_x // 4, cells_y // 4
        self.tiles = self.tx * self.ty
        self.head, self.outc = head, outc
        self.colp = pad16(cells_x)
        self.rows = 9 * channels
        self.rc = self.rows // 2
        self.ra = self.rc // 2
        self.az = self.ra // self.Z
        self.azp = pad16(self.az)
        self.bx = self.ra // self.X
        self.rl = self.az // self.X
        self.rlp = pad16(self.rl)
        self.nb = self.Y // 2
        self.hb = 2 * self.rl // self.nb
        self.hbp = pad16(self.hb)
        self.hrows = (channels * head + head * outc) // channels
        self.hc = self.hrows // 2
        self.hx = self.hc // self.X
        self.hz = self.hx // self.Z
        self.hzp = pad16(self.hz)
        self.scale = 1.0 / math.sqrt(n_src * n_gx * n_gy * cells_x * cells_y)


def kernel(
    d,
    cam, lidar_h, act_h, tsrc_h, wconv_h, hup_h, hout_h, cot_h,
    maps_o, gin_o, gcam_o, gconv_o, gup_o, gout_o,
    arrived, lidar, wconv, hup, hout, cot, act, tvec, tsrc, inv_v, inv,
    wt, hup_t, hout_t, mask,
    m32, m3, g3, rows_s, rows_r, cols_s, cols_r,
    feat, hid, gh, maps, gp, gi, tiles, ret,
    dw32, dwb, core_r, cs32,
    az, az_r, azsum, ax32, ax, ax_r, ahrow,
    bx, bx_r, bxsum, bz32, bz, bz_r, bhrow, ls, l_r,
    h32, hb, hcore_r, hs32, hxs, hx_r, hxsum, hzs32, hzs, hz_r, hy, hy_r, hpart, hpack, hall,
    in_sem, out_sem,
    a_send, a_recv, b_send, b_recv, row_send, row_recv, col_send, col_recv, core_send, core_recv,
    az_send, az_recv, ax_send, ax_recv, bx_send, bx_recv, bz_send, bz_recv, l_send, l_recv,
    hx_send, hx_recv, hz_send, hz_recv, hy_send, hy_recv, gz_send, gz_recv, gx_send, gx_recv,
):
    s = lax.axis_index("src")
    g = lax.axis_index("gx")
    r = lax.axis_index("gy")
    core, yl = g % 2, g // 2
    z, yh = r // 2, r % 2
    me = s * d.GX + g
    X, Y, Z, N, C, CY = d.X, d.Y, d.Z, d.N, d.c, d.cy

    loads = [
        pltpu.make_async_copy(src, dst, in_sem.at[k])
        for k, (src, dst) in enumerate(
            [(act_h, act), (tsrc_h, tvec), (tsrc_h, tsrc), (wconv_h, wconv), (hup_h, hup),
             (hout_h, hout), (lidar_h, lidar), (cot_h, cot), (cam.at[me], arrived.at[me])]
        )
    ]

    order = {1: (0,), 2: (1, 0)}.get(d.YL) or (d.YL // 2, *[k for k in range(1, d.YL) if k != d.YL // 2], 0)

    def a_peer(far, step):
        to_s = (s + step // 2) % X
        to_g = ((yl + far) % d.YL) * 2 + (core + step) % 2
        return to_s * d.GX + to_g, (to_s, to_g, r)

    def each_peer(body):
        for far in order:
            lax.fori_loop(0 if far else 1, 2 * X, lambda step, _, far=far: body(far, step) or 0, 0)

    def z_peer(step):
        return (s, g, ((z + step) % Z) * 2 + yh)

    def x_peer(step):
        return ((s + step) % X, g, r)

    def y_peer(step):
        at = (yl * 2 + yh + step) % Y
        return (s, (at // 2) * 2 + core, z * 2 + at % 2)

    other_core = (s, yl * 2 + 1 - core, r)

    my_block = (s * d.GX + g) * d.GY + r
    per_half = Z * X * d.nb
    from_core = my_block // (2 * per_half)
    from_b = (my_block // per_half) % 2
    place = (my_block % per_half) // d.nb
    from_z = jnp.where(from_b == 1, place % Z, place // X)
    from_x = jnp.where(from_b == 1, place // Z, place % X)
    my_y = yl * 2 + yh

    def block_of(half, k):
        where = z * X + s if half == 0 else s * Z + z
        return (core * 2 + half) * per_half + where * d.nb + k

    def owner(block):
        return (block // (d.GX * d.GY), (block // d.GY) % d.GX, block % d.GY)

    def last_sender(at):
        return (from_x, (at // 2) * 2 + from_core, from_z * 2 + at % 2)

    self_group = jnp.logical_and(
        jnp.logical_and(from_core == core, from_z == z), from_x == s
    )

    barrier = pltpu.get_barrier_semaphore()

    def greet(device):
        pl.semaphore_signal(barrier, inc=1, device_id=device, device_id_type=MESH)

    each_peer(lambda far, step: greet(a_peer(far, step)[1]))
    count = N - 1
    for step in range(1, Z):
        greet(z_peer(step))
        count += 1
    for at in range(d.YL):
        greet((s, at * 2 + core, z * 2 + 1 - yh))
        count += 1
    for side in (-1, 1):
        for near in (-1, 0, 1):
            greet((s, (g + near + d.GX) % d.GX, (r + side + d.GY) % d.GY))
            count += 1
    for at in range(Y):
        is_self = jnp.logical_and(self_group, my_y == at)

        @pl.when(jnp.logical_not(is_self))
        def _():
            greet(last_sender(at))

    count = count + Y - jnp.where(self_group, 1, 0)
    pl.semaphore_wait(barrier, count)

    def a_start(far, step):
        to, device = a_peer(far, step)
        rcopy(cam.at[to], arrived.at[me], a_send, a_recv, device).start()

    each_peer(a_start)
    for load in loads:
        load.start()

    for load in loads[:6]:
        load.wait()
    at_y = lax.broadcasted_iota(jnp.int32, (CY, d.ty), 0) // 4
    at_q = lax.broadcasted_iota(jnp.int32, (CY, d.ty), 1)
    for p in range(d.tx):
        row = act[p : p + 1, :].astype(F32)
        column = jnp.sum(jnp.where(at_y == at_q, row, 0.0), axis=1, keepdims=True)
        mask[p] = jnp.broadcast_to(column, (CY, C))
    eye = lax.broadcasted_iota(jnp.int32, (d.ty, d.ty), 0) == lax.broadcasted_iota(
        jnp.int32, (d.ty, d.ty), 1
    )
    at_t = lax.broadcasted_iota(jnp.int32, (d.ty, 128), 0)
    at_s = lax.broadcasted_iota(jnp.int32, (d.ty, 128), 1)
    found = jnp.zeros((1, 128), jnp.int32)
    for p in range(d.tx):
        column = jnp.sum(jnp.where(eye, tvec[p : p + 1, :], 0), axis=1, keepdims=True)
        hit = jnp.where(column == at_s, at_t + p * d.ty, 0)
        found = jnp.maximum(found, jnp.max(hit, axis=0, keepdims=True))
    inv_v[...] = jnp.broadcast_to(found, (8, 128))
    inv_copy = pltpu.make_async_copy(inv_v, inv, in_sem.at[0])
    inv_copy.start()
    for i in range(3):
        for j in range(3):
            tap = wconv[2 - i, (2 - j) * C : (3 - j) * C, :].astype(F32)
            wt[i, j * C : (j + 1) * C, :] = tap.T.astype(BF16)
    hup_t[...] = hup[...].astype(F32).T.astype(BF16)
    hout_t[...] = hout[...].astype(F32).T.astype(BF16)

    inv_copy.wait()
    for load in loads[6:]:
        load.wait()
    all_but_one = pl.ds(0, N - 1)
    rcopy(
        arrived.at[all_but_one], arrived.at[all_but_one], a_send, a_recv, other_core
    ).wait_recv()

    span = 4 * CY

    def merge(p, _):
        for q in range(d.ty):
            at = tsrc[p, q]
            tile = arrived[at // 2, at % 2].astype(F32)
            for dx in range(4):
                m32[4 * p + dx, 4 * q : 4 * q + 4, :] = tile[4 * dx : 4 * dx + 4]
        for dx in range(4):
            x = 4 * p + dx
            line = pl.ds(pl.multiple_of(x * CY, CY), CY)
            m32[x] = mask[p] * (m32[x] + lidar[line, :].astype(F32))
        return 0

    lax.fori_loop(0, d.tx, merge, 0)

    def send_all(parts, slots, size, here, peer, send_sem, recv_sem):
        for k in range(1, size):
            rcopy(parts.at[(here + k) % size], slots.at[k - 1], send_sem, recv_sem, peer(k)).start()
        return rcopy(slots, slots, send_sem, recv_sem, other_core)

    def halo_start(k):
        rows_s[k, 0] = m32[0].astype(BF16)
        rows_s[k, 1] = m32[d.cx - 1].astype(BF16)
        cols_s[k, 0, 0 : d.cx, :] = m32[:, 0, :].astype(BF16)
        cols_s[k, 1, 0 : d.cx, :] = m32[:, CY - 1, :].astype(BF16)
        for side, step in ((0, -1), (1, 1)):
            for near in (-1, 0, 1):
                device = (s, (g + near + d.GX) % d.GX, (r + step + d.GY) % d.GY)
                rcopy(
                    cols_s.at[k, side], cols_r.at[k, 1 - side, 1 - near], col_send.at[k],
                    col_recv.at[k], device,
                ).start()
            device = (s, (g + step + d.GX) % d.GX, r)
            rcopy(
                rows_s.at[k, side], rows_r.at[k, 1 - side], row_send.at[k], row_recv.at[k], device
            ).start()

    at_row = lax.broadcasted_iota(jnp.int32, (CY, C), 0)
    head_row = lax.broadcasted_iota(jnp.int32, (16, C), 0)

    def put(out3, x, line, left, right):
        down = jnp.where(at_row == 0, left, pltpu.roll(line, 1, 0))
        up = jnp.where(at_row == CY - 1, right, pltpu.roll(line, CY - 1, 0))
        out3[x * CY : (x + 1) * CY, 0:C] = down.astype(BF16)
        out3[x * CY : (x + 1) * CY, C : 2 * C] = line.astype(BF16)
        out3[x * CY : (x + 1) * CY, 2 * C : 3 * C] = up.astype(BF16)

    def put_ends(out3, x, left, right):
        top = m32[x - 1, 0:16, :]
        low = m32[x - 1, CY - 16 : CY, :]
        down = jnp.where(head_row == 0, left, pltpu.roll(top, 1, 0))
        up = jnp.where(head_row == 15, right, pltpu.roll(low, 15, 0))
        out3[x * CY : x * CY + 16, 0:C] = down.astype(BF16)
        out3[(x + 1) * CY - 16 : (x + 1) * CY, 2 * C : 3 * C] = up.astype(BF16)

    def halo_inner(out3):
        for x in range(d.cx):
            put(out3, x + 1, m32[x], 0.0, 0.0)

    def halo_finish(k, out3, ends):
        rcopy(rows_s.at[k], rows_r.at[k], row_send.at[k], row_recv.at[k], other_core).wait_recv()
        rcopy(cols_r.at[k], cols_r.at[k], col_send.at[k], col_recv.at[k], other_core).wait_recv()
        ok_g = (g > 0, g < d.GX - 1)
        ok_r = (r > 0, r < d.GY - 1)
        lefts = [jnp.where(ok_r[0], cols_r[k, 0, near].astype(F32), 0.0) for near in range(3)]
        rights = [jnp.where(ok_r[1], cols_r[k, 1, near].astype(F32), 0.0) for near in range(3)]
        for side, x, row in ((0, 0, d.cx - 1), (1, d.cx + 1, 0)):
            line = rows_r[k, side].astype(F32)
            near = 0 if side == 0 else 2
            line, left, right = [
                jnp.where(ok_g[side], value, 0.0)
                for value in (line, lefts[near][row : row + 1], rights[near][row : row + 1])
            ]
            put(out3, x, line, left, right)
        for x in range(d.cx):
            left, right = lefts[1][x : x + 1], rights[1][x : x + 1]
            if ends:
                put_ends(out3, x + 1, left, right)
            else:
                put(out3, x + 1, m32[x], left, right)

    halo_start(0)
    halo_inner(m3)
    halo_finish(0, m3, True)

    def forward(p, _):
        here = pl.ds(pl.multiple_of(p * span, span), span)
        pre = jnp.zeros((span, C), F32)
        for i in range(3):
            pre = pre + dot(
                m3[pl.ds(pl.multiple_of(p * span + i * CY, CY), span), :], wconv[i]
            )
        occupied = jnp.concatenate([mask[p]] * 4, axis=0)
        sig = sigmoid(pre)
        feature = (occupied * (pre * sig)).astype(BF16)
        slope = occupied * (sig * (1.0 + pre * (1.0 - sig)))
        feat[here, :] = feature
        lines = pl.ds(4 * p, 4)
        m32[lines] = slope.reshape(4, CY, C)
        up = dot(feature, hup[...])
        sig = sigmoid(up)
        hidden = (up * sig).astype(BF16)
        hid[here, :] = hidden
        maps[here, :] = dot(hidden, hout[...]).astype(BF16)
        grad = (dot(cot[here, :], hout_t[...]) * (sig * (1.0 + up * (1.0 - sig)))).astype(BF16)
        gh[here, :] = grad
        value = dot(grad, hup_t[...]) * m32[lines].reshape(span, C)
        m32[lines] = value.reshape(4, CY, C)
        gp[here, :] = value.astype(BF16)
        return 0

    lax.fori_loop(0, d.tx, forward, 0)
    halo_start(1)
    maps_out = pltpu.make_async_copy(maps, maps_o, out_sem.at[0])
    maps_out.start()

    def last(half, total, rows):
        rows[pl.ds(0, d.rlp, stride=2), :] = total[:, 0:128]
        rows[pl.ds(1, d.rlp, stride=2), :] = total[:, 128:256]
        for k in range(d.nb):
            at = half * d.nb + k
            ls[at] = rows[k * d.hb : k * d.hb + d.hbp, :].astype(BF16)
            block = block_of(half, k)
            copy = rcopy(ls.at[at], l_r.at[my_y], l_send, l_recv, owner(block))
            local = pltpu.make_async_copy(ls.at[at], l_r.at[my_y], l_recv)

            @pl.when(block != my_block)
            def _():
                copy.start()

            @pl.when(block == my_block)
            def _():
                local.start()

    term = dot_tn(feat[...], gh[...])
    for half in range(d.head // C):
        h32[half * C : (half + 1) * C, :] = term[:, half * C : (half + 1) * C]
    base = d.head
    term = dot_tn(hid[...], cot[...])
    depth = d.head // 2
    for half in range(2):
        h32[base : base + depth, half * d.outc : (half + 1) * d.outc] = term[
            half * depth : (half + 1) * depth, :
        ]
    hb[...] = h32[...].astype(BF16)
    hmine = pl.ds(pl.multiple_of(core * d.hc, d.hc), d.hc)
    htheirs = pl.ds(pl.multiple_of((1 - core) * d.hc, d.hc), d.hc)
    hcore_copy = rcopy(hb.at[htheirs], hcore_r, core_send.at[1], core_recv.at[1], other_core)
    hcore_copy.start()

    def tap_grads(i, _):
        for j in range(3):
            term = dot_tn(
                m3[pl.ds(pl.multiple_of(i * CY, CY), d.cells), j * C : (j + 1) * C], gp[...]
            )
            at = pl.ds(pl.multiple_of(i * (3 * C) + j * C, C), C)
            dw32[at, :] = term
            dwb[at, :] = term.astype(BF16)
        return 0

    lax.fori_loop(0, 3, tap_grads, 0)
    mine = pl.ds(pl.multiple_of(core * d.rc, d.rc), d.rc)
    theirs = pl.ds(pl.multiple_of((1 - core) * d.rc, d.rc), d.rc)
    core_copy = rcopy(dwb.at[theirs], core_r, core_send.at[0], core_recv.at[0], other_core)
    core_copy.start()

    hcore_copy.wait_recv()
    hs32[...] = h32[hmine, :] + hcore_r[...].astype(F32)
    for k in range(X):
        hxs[k] = hs32[k * d.hx : (k + 1) * d.hx, :].astype(BF16)
    hx_wait = send_all(hxs, hx_r, X, s, x_peer, hx_send, hx_recv)

    halo_finish(1, g3, False)

    hx_wait.wait_recv()
    total = hs32[pl.ds(pl.multiple_of(s * d.hx, d.hx), d.hx), :]
    for k in range(X - 1):
        total = total + hx_r[k].astype(F32)
    hxsum[0 : d.hx, :] = total
    for k in range(Z):
        part = hxsum[k * d.hz : k * d.hz + d.hzp, :]
        hzs32[k] = part
        hzs[k] = part.astype(BF16)
    hz_wait = send_all(hzs, hz_r, Z, z, z_peer, hz_send, hz_recv)

    core_copy.wait_recv()
    cs32[...] = dw32[mine, :] + core_r[...].astype(F32)
    for k in range(Z):
        az[k] = cs32[k * d.az : k * d.az + d.azp, :].astype(BF16)
    az_wait = send_all(az, az_r, Z, z, z_peer, az_send, az_recv)
    for k in range(X):
        bx[k] = cs32[d.ra + k * d.bx : d.ra + (k + 1) * d.bx, :].astype(BF16)
    bx_wait = send_all(bx, bx_r, X, s, x_peer, bx_send, bx_recv)

    def backward(p, _):
        here = pl.ds(pl.multiple_of(p * span, span), span)
        acc = jnp.zeros((span, C), F32)
        for i in range(3):
            acc = acc + dot(g3[pl.ds(pl.multiple_of(p * span + i * CY, CY), span), :], wt[i])
        acc = acc * jnp.concatenate([mask[p]] * 4, axis=0)
        gi[here, :] = acc.astype(BF16)
        m32[pl.ds(4 * p, 4)] = acc.reshape(4, CY, C)
        for q in range(d.ty):
            parts = [m32[4 * p + dx, 4 * q : 4 * q + 4, :] for dx in range(4)]
            tiles[p * d.ty + q] = jnp.concatenate(parts, axis=0).astype(BF16)
        return 0

    lax.fori_loop(0, d.tx, backward, 0)
    gin_out = pltpu.make_async_copy(gi, gin_o, out_sem.at[1])
    gin_out.start()

    hz_wait.wait_recv()
    total = hzs32[z]
    for k in range(Z - 1):
        total = total + hz_r[k].astype(F32)
    hy[...] = total.astype(BF16)
    for k in range(1, Y):
        rcopy(hy, hy_r.at[k - 1], hy_send, hy_recv, y_peer(k)).start()
    hy_wait = rcopy(hy_r, hy_r, hy_send, hy_recv, other_core)

    def b_start(far, step):
        to, device = a_peer(far, step)
        for slot in range(2):
            ret[to, slot] = tiles[inv[0, to * 2 + slot]]
        rcopy(ret.at[to], gcam_o.at[me], b_send, b_recv, device).start()

    each_peer(b_start)
    for slot in range(2):
        ret[me, slot] = tiles[inv[0, me * 2 + slot]]
    own_out = pltpu.make_async_copy(ret.at[me], gcam_o.at[me], out_sem.at[2])
    own_out.start()

    bx_wait.wait_recv()
    total = cs32[pl.ds(pl.multiple_of(d.ra + s * d.bx, 8), d.bx), :]
    for k in range(X - 1):
        total = total + bx_r[k].astype(F32)
    bxsum[0 : d.bx, :] = total
    for k in range(Z):
        part = bxsum[k * d.rl : k * d.rl + d.rlp, :]
        bz32[k] = part
        bz[k] = part.astype(BF16)
    bz_wait = send_all(bz, bz_r, Z, z, z_peer, bz_send, bz_recv)

    hy_wait.wait_recv()
    total = hy[...].astype(F32)
    for k in range(Y - 1):
        total = total + hy_r[k].astype(F32)
    hpart[z] = total.astype(BF16)
    part = hpart.at[z]
    for k in range(1, Z):
        rcopy(part, part, gz_send, gz_recv, z_peer(k)).start()

    az_wait.wait_recv()
    total = cs32[pl.ds(pl.multiple_of(z * d.az, 8), d.azp), :]
    for k in range(Z - 1):
        total = total + az_r[k].astype(F32)
    azsum[0 : d.azp, :] = total
    for k in range(X):
        part = azsum[k * d.rl : k * d.rl + d.rlp, :]
        ax32[k] = part
        ax[k] = part.astype(BF16)
    ax_wait = send_all(ax, ax_r, X, s, x_peer, ax_send, ax_recv)

    parts = hpart.at[pl.ds(0, Z - 1)]
    gz_wait = rcopy(parts, parts, gz_send, gz_recv, other_core)
    gz_wait.wait_recv()
    for k in range(Z):
        hpack[k * d.hz : k * d.hz + d.hzp, :] = hpart[k].astype(F32)
    hall[core, s] = hpack[0 : d.hx, :].astype(BF16)
    part = hall.at[core, s]
    for k in range(1, X):
        rcopy(part, part, gx_send, gx_recv, x_peer(k)).start()

    bz_wait.wait_recv()
    total = bz32[z]
    for k in range(Z - 1):
        total = total + bz_r[k].astype(F32)
    last(1, total, bhrow)
    ax_wait.wait_recv()
    total = ax32[s]
    for k in range(X - 1):
        total = total + ax_r[k].astype(F32)
    last(0, total, ahrow)

    parts = hall.at[core, pl.ds(0, X - 1)]
    gx_wait = rcopy(parts, parts, gx_send, gx_recv, other_core)
    gx_wait.wait_recv()
    gcore = rcopy(hall.at[core], hall.at[core], core_send.at[2], core_recv.at[2], other_core)
    gcore.start()

    total = jnp.zeros((d.hbp, 128), F32)
    pltpu.make_async_copy(ls, l_r, l_recv).wait()
    for k in range(Y):
        total = total + l_r[k].astype(F32)
    gconv_o[...] = total[0 : d.hb, :] * d.scale

    rcopy(
        hall.at[1 - core], hall.at[1 - core], core_send.at[2], core_recv.at[2], other_core
    ).wait_recv()
    for c in range(2):
        for x in range(X):
            at = c * d.hc + x * d.hx
            h32[at : at + d.hx, :] = hall[c, x].astype(F32)
    for half in range(d.head // C):
        gup_o[:, half * C : (half + 1) * C] = h32[half * C : (half + 1) * C, :] * d.scale
    for half in range(2):
        gout_o[half * depth : (half + 1) * depth, :] = (
            h32[base : base + depth, half * d.outc : (half + 1) * d.outc] * d.scale
        )

    parts = ret.at[all_but_one]
    b_wait = rcopy(parts, gcam_o.at[all_but_one], b_send, b_recv, other_core)
    b_wait.wait_recv()

    rcopy(parts, parts, a_send, a_recv, other_core).wait_send()
    b_wait.wait_send()
    for k in range(2):
        rcopy(rows_s.at[k], rows_r.at[k], row_send.at[k], row_recv.at[k], other_core).wait_send()
        rcopy(cols_r.at[k], cols_r.at[k], col_send.at[k], col_recv.at[k], other_core).wait_send()
    for wait in (
        az_wait, ax_wait, bx_wait, bz_wait, hx_wait, hz_wait, hy_wait, gz_wait, gx_wait,
        core_copy, hcore_copy, gcore,
    ):
        wait.wait_send()

    @pl.when(self_group)
    def _():
        parts = ls.at[pl.ds(0, Y - 1)]
        rcopy(parts, parts, l_send, l_recv, other_core).wait_send()

    @pl.when(jnp.logical_not(self_group))
    def _():
        rcopy(ls, ls, l_send, l_recv, other_core).wait_send()

    maps_out.wait()
    gin_out.wait()
    own_out.wait()


def copy_kernel(*refs):
    loads = [
        pltpu.make_async_copy(refs[k], refs[12 + k], refs[18].at[k]) for k in range(6)
    ]
    stores = [
        pltpu.make_async_copy(refs[12 + k], refs[6 + k], refs[18].at[k]) for k in range(6)
    ]
    for load in loads:
        load.start()
    for load, store in zip(loads, stores):
        load.wait()
        store.start()
    for store in stores:
        store.wait()


def per_device(
    cam_send, lidar_bev, tile_active, tile_source, conv_weight, head_up, head_out, cotangent
):
    channels = cam_send.shape[5]
    cells_x, cells_y = lidar_bev.shape[1], lidar_bev.shape[2]
    head, outc = head_out.shape
    d = Dims(
        lax.axis_size("src"), lax.axis_size("gx"), lax.axis_size("gy"),
        cells_x, cells_y, channels, head, outc,
    )
    C, X, Y, Z, N = d.c, d.X, d.Y, d.Z, d.N
    cells = d.cells
    vmem = pl.BlockSpec(memory_space=pltpu.VMEM)
    anyw = pl.BlockSpec(memory_space=pl.ANY)
    dma = pltpu.SemaphoreType.DMA

    def b16(*shape):
        return pltpu.VMEM(shape, BF16)

    def f32(*shape):
        return pltpu.VMEM(shape, F32)

    def i32(*shape):
        return pltpu.VMEM(shape, jnp.int32)

    scratch = [
        b16(N, 2, 16, C), b16(cells, C), b16(3, 3 * C, C), b16(C, head), b16(head, outc),
        b16(cells, outc), i32(d.tx, d.ty), i32(d.tx, d.ty), pltpu.SMEM((d.tx, d.ty), jnp.int32),
        i32(8, 128), pltpu.SMEM((8, 128), jnp.int32),
        b16(3, 3 * C, C), b16(head, C), b16(outc, head), f32(d.tx, cells_y, C),
        f32(cells_x, cells_y, C), b16((cells_x + 2) * cells_y, 3 * C), b16((cells_x + 2) * cells_y, 3 * C),
        b16(2, 2, cells_y, C), b16(2, 2, cells_y, C),
        b16(2, 2, d.colp, C), b16(2, 2, 3, d.colp, C),
        b16(cells, C), b16(cells, head), b16(cells, head), b16(cells, outc), b16(cells, C),
        b16(cells, C), b16(d.tiles, 16, C), b16(N, 2, 16, C),
        f32(d.rows, C), b16(d.rows, C), b16(d.rc, C), f32(d.rc, C),
        b16(Z, d.azp, C), b16(Z - 1, d.azp, C), f32(d.azp + d.rlp, C),
        f32(X, d.rlp, C), b16(X, d.rlp, C), b16(X - 1, d.rlp, C), f32(2 * d.rlp, 128),
        b16(X, d.bx, C), b16(X - 1, d.bx, C), f32(d.bx + d.rlp, C),
        f32(Z, d.rlp, C), b16(Z, d.rlp, C), b16(Z - 1, d.rlp, C), f32(2 * d.rlp, 128),
        b16(Y, d.hbp, 128), b16(Y, d.hbp, 128),
        f32(d.hrows, C), b16(d.hrows, C), b16(d.hc, C), f32(d.hc, C),
        b16(X, d.hx, C), b16(X - 1, d.hx, C), f32(d.hx + 16, C),
        f32(Z, d.hzp, C), b16(Z, d.hzp, C), b16(Z - 1, d.hzp, C),
        b16(d.hzp, C), b16(Y - 1, d.hzp, C),
        b16(Z, d.hzp, C), f32(d.hx + 16, C), b16(2, X, d.hx, C),
        dma((9,)), dma((3,)),
        dma, dma, dma, dma, dma((2,)), dma((2,)), dma((2,)), dma((2,)), dma((3,)), dma((3,)),
        *[dma] * 20,
    ]
    results = pl.pallas_call(
        functools.partial(kernel, d),
        out_shape=(
            jax.ShapeDtypeStruct((cells, outc), BF16),
            jax.ShapeDtypeStruct((cells, C), BF16),
            jax.ShapeDtypeStruct((N, 2, 16, C), BF16),
            jax.ShapeDtypeStruct((d.hb, 128), F32),
            jax.ShapeDtypeStruct((C, head), F32),
            jax.ShapeDtypeStruct((head, outc), F32),
        ),
        in_specs=[anyw] * 8,
        out_specs=(anyw, anyw, anyw, vmem, vmem, vmem),
        scratch_shapes=scratch,
        compiler_params=pltpu.CompilerParams(
            collective_id=0, has_side_effects=True, vmem_limit_bytes=64 * 1024 * 1024
        ),
    )(
        cam_send.reshape(N, 2, 16, C),
        lidar_bev.reshape(cells, C),
        tile_active.reshape(d.tx, d.ty),
        tile_source.reshape(d.tx, d.ty),
        conv_weight.reshape(3, 3 * C, C),
        head_up,
        head_out,
        cotangent.reshape(cells, outc),
    )
    maps, gin, gcam, gconv, gup, gout = pl.pallas_call(
        copy_kernel,
        out_shape=tuple(jax.ShapeDtypeStruct(a.shape, a.dtype) for a in results),
        in_specs=[anyw] * 6,
        out_specs=(anyw,) * 6,
        scratch_shapes=[*[pltpu.VMEM(a.shape, a.dtype) for a in results], dma((6,))],
        compiler_params=pltpu.CompilerParams(vmem_limit_bytes=64 * 1024 * 1024),
    )(*results)
    return (
        maps.reshape(1, cells_x, cells_y, outc),
        gin.reshape(1, cells_x, cells_y, C),
        gcam.reshape(1, 1, N, 2, 16, C),
        gconv.reshape(-1),
        gup,
        gout,
    )


def solution(mesh):
    in_specs = (
        P(("src", "gx"), "gy", None, None, None, None),
        P("src", "gx", "gy", None),
        P("src", "gx", "gy"),
        P("src", "gx", "gy"),
        P(),
        P(),
        P(),
        P("src", "gx", "gy", None),
    )
    out_specs = (
        P("src", "gx", "gy", None),
        P("src", "gx", "gy", None),
        P(("src", "gx"), "gy", None, None, None, None),
        P(("src", "gx", "gy")),
        P(),
        P(),
    )
    return jax.shard_map(
        per_device, mesh=mesh, in_specs=in_specs, out_specs=out_specs, check_vma=False
    )
```

time: 99.7 us -> 80.2 us (0.80)
  local copies, waits for them, and re-layouts: 12.7 us -> 0 us
  Pallas kernels: 85.4 us -> 78.9 us
    unnamed x22 -> x0, local copies, waits for them, and re-layouts: 11.9 us -> none
    pallas_call x1, Pallas kernels: 85.4 us -> 76.5 us  [per_device(): pl.pallas_call(functools.partial(kernel, d), out_shape=(jax.ShapeDtypeStr...]
    pallas_call x0 -> x1, Pallas kernels: none -> 2.4 us  [per_device(): pl.pallas_call(copy_kernel, out_shape=tuple((jax.ShapeDtypeStruct(a.shape...]
where the time goes in v2:
time: 80.2 us; the launch traced here: 79.5 us
  Pallas kernels  78.9 us (98%)
    pallas_call x1, Pallas kernels, per_device(): pl.pallas_call(functools.partial(kernel, d), out_shape=(jax.ShapeDtypeStr...  76.5 us
    pallas_call x1, Pallas kernels, per_device(): pl.pallas_call(copy_kernel, out_shape=tuple((jax.ShapeDtypeStruct(a.shape...  2.4 us

profile of v2, /device:TPU:1, one launch (start us, length us, event | category | flops | bytes accessed | tf_op | source)
XLA Modules:
  0.0 79.5 jit_solution(8608672571958549783)
XLA Ops:
  0.6 76.5 %shard_map.127 = (bf16[1024,128]{1,0:T(8,128)(2,1)}, bf16[1024,256]{1,0:T(8,128)(2,1)}, bf16[32,2,16,256]{3,2,1,0:T(8,128)(2,1)}, f32[9,128]{1,0:T(8,128)}, f32[256,512]{1,0:T(8,128)}, /*index=5*/f32[512,128]{1,0:T(8,128)}) custom-call(bf16[32,2,16,256]{3,2,1,0:T(8,128)(2,1)} %bitcast.11, bf16[1024,256]{1,0:T(8,128)(2,1)} %bitcast.12, s32[4,16]{1,0:T(4,128)} %bitcast.14, ...), custom_call_target="tpu_custom_call" | custom-call | tf_op jit(solution)/shard_map/pallas_call | solution.py:629
  77.1 2.4 %shard_map.128 = (bf16[1024,128]{1,0:T(8,128)(2,1)}, bf16[1024,256]{1,0:T(8,128)(2,1)}, bf16[32,2,16,256]{3,2,1,0:T(8,128)(2,1)}, f32[9,128]{1,0:T(8,128)}, f32[256,512]{1,0:T(8,128)}, /*index=5*/f32[512,128]{1,0:T(8,128)}) custom-call(bf16[1024,128]{1,0:T(8,128)(2,1)} %get-tuple-element.18.refs_0_, bf16[1024,256]{1,0:T(8,128)(2,1)} %get-tuple-element.19.refs_1_, ...), custom_call_target="tpu_custom_call" | custom-call | tf_op jit(solution)/shard_map/pallas_call | solution.py:655

commit v3 on v2

--- a/solution.py
+++ b/solution.py
@@ -53,14 +53,10 @@
         self.colp = pad16(cells_x)
         self.rows = 9 * channels
         self.rc = self.rows // 2
-        self.ra = self.rc // 2
-        self.az = self.ra // self.Z
-        self.azp = pad16(self.az)
-        self.bx = self.ra // self.X
-        self.rl = self.az // self.X
+        self.bx = self.rc // self.X
+        self.rl = self.bx // self.Z
         self.rlp = pad16(self.rl)
-        self.nb = self.Y // 2
-        self.hb = 2 * self.rl // self.nb
+        self.hb = 2 * self.rl // self.Y
         self.hbp = pad16(self.hb)
         self.hrows = (channels * head + head * outc) // channels
         self.hc = self.hrows // 2
@@ -76,15 +72,14 @@
     maps_o, gin_o, gcam_o, gconv_o, gup_o, gout_o,
     arrived, lidar, wconv, hup, hout, cot, act, tvec, tsrc, inv_v, inv,
     wt, hup_t, hout_t, mask,
-    m32, m3, g3, rows_s, rows_r, cols_s, cols_r,
+    m32, conv, m3, g3, rows_s, rows_r, cols_s, cols_r,
     feat, hid, gh, maps, gp, gi, tiles, ret,
     dw32, dwb, core_r, cs32,
-    az, az_r, azsum, ax32, ax, ax_r, ahrow,
-    bx, bx_r, bxsum, bz32, bz, bz_r, bhrow, ls, l_r,
+    bx, bx_r, bxsum, bz32, bz, bz_r, brow, ls, l_r,
     h32, hb, hcore_r, hs32, hxs, hx_r, hxsum, hzs32, hzs, hz_r, hy, hy_r, hpart, hpack, hall,
     in_sem, out_sem,
     a_send, a_recv, b_send, b_recv, row_send, row_recv, col_send, col_recv, core_send, core_recv,
-    az_send, az_recv, ax_send, ax_recv, bx_send, bx_recv, bz_send, bz_recv, l_send, l_recv,
+    bx_send, bx_recv, bz_send, bz_recv, l_send, l_recv,
     hx_send, hx_recv, hz_send, hz_recv, hy_send, hy_recv, gz_send, gz_recv, gx_send, gx_recv,
 ):
     s = lax.axis_index("src")
@@ -103,16 +98,28 @@
         )
     ]
 
-    order = {1: (0,), 2: (1, 0)}.get(d.YL) or (d.YL // 2, *[k for k in range(1, d.YL) if k != d.YL // 2], 0)
+    order = (3, 2, 1, 0) if d.YL == 4 else range(d.YL - 1, -1, -1)
 
     def a_peer(far, step):
         to_s = (s + step // 2) % X
-        to_g = ((yl + far) % d.YL) * 2 + (core + step) % 2
+        if d.YL == 4:
+            to_yl = {3: 3 - yl, 2: (yl + 2) % 4, 1: yl + 1 - 2 * (yl % 2), 0: yl}[far]
+        else:
+            to_yl = (yl + far) % d.YL
+        to_g = to_yl * 2 + (core + step) % 2
         return to_s * d.GX + to_g, (to_s, to_g, r)
 
     def each_peer(body):
         for far in order:
-            lax.fori_loop(0 if far else 1, 2 * X, lambda step, _, far=far: body(far, step) or 0, 0)
+            if far:
+                body(far, 0)
+
+        def rest(step, _):
+            for far in order:
+                body(far, step)
+            return 0
+
+        lax.fori_loop(1, 2 * X, rest, 0)
 
     def z_peer(step):
         return (s, g, ((z + step) % Z) * 2 + yh)
@@ -127,17 +134,10 @@
     other_core = (s, yl * 2 + 1 - core, r)
 
     my_block = (s * d.GX + g) * d.GY + r
-    per_half = Z * X * d.nb
-    from_core = my_block // (2 * per_half)
-    from_b = (my_block // per_half) % 2
-    place = (my_block % per_half) // d.nb
-    from_z = jnp.where(from_b == 1, place % Z, place // X)
-    from_x = jnp.where(from_b == 1, place // Z, place % X)
+    group = my_block // Y
+    from_core, from_x, from_z = group // (X * Z), (group // Z) % X, group % Z
     my_y = yl * 2 + yh
-
-    def block_of(half, k):
-        where = z * X + s if half == 0 else s * Z + z
-        return (core * 2 + half) * per_half + where * d.nb + k
+    first_block = ((core * X + s) * Z + z) * Y
 
     def owner(block):
         return (block // (d.GX * d.GY), (block // d.GY) % d.GX, block % d.GY)
@@ -299,20 +299,46 @@
             left, right = lefts[1][x : x + 1], rights[1][x : x + 1]
             if ends:
                 put_ends(out3, x + 1, left, right)
-            else:
-                put(out3, x + 1, m32[x], left, right)
+
+    def conv_inner(from3, weight):
+        from3[0:CY, :] = jnp.zeros((CY, 3 * C), BF16)
+        from3[(d.cx + 1) * CY :, :] = jnp.zeros((CY, 3 * C), BF16)
+
+        def chunk(p, _):
+            acc = jnp.zeros((span, C), F32)
+            for i in range(3):
+                start = pl.multiple_of(p * span + i * CY, CY)
+                acc = acc + dot(from3[pl.ds(start, span), :], weight[i])
+            conv[pl.ds(4 * p, 4)] = acc.reshape(4, CY, C)
+            return 0
+
+        lax.fori_loop(0, d.tx, chunk, 0, unroll=True)
+
+    def conv_edges(k, from3, weight):
+        conv[0] = conv[0] + dot(from3[0:CY, :], weight[0])
+        conv[d.cx - 1] = conv[d.cx - 1] + dot(from3[(d.cx + 1) * CY :, :], weight[2])
+        at = lax.broadcasted_iota(jnp.int32, (d.colp, C), 0)
+        for side, y, ok in ((0, 0, r > 0), (1, CY - 1, r < d.GY - 1)):
+            line = cols_r[k, side, 1].astype(F32)
+            line = jnp.where(jnp.logical_and(ok, at < d.cx), line, 0.0).astype(BF16)
+            tap = 2 * side
+            before, here, after = [
+                dot(line, weight[i, tap * C : (tap + 1) * C, :]) for i in range(3)
+            ]
+            before = jnp.where(at == 0, 0.0, pltpu.roll(before, 1, 0))
+            after = jnp.where(at == d.colp - 1, 0.0, pltpu.roll(after, d.colp - 1, 0))
+            total = before + here + after
+            conv[:, y, :] = conv[:, y, :] + total[0 : d.cx]
 
     halo_start(0)
     halo_inner(m3)
+    conv_inner(m3, wconv)
     halo_finish(0, m3, True)
+    conv_edges(0, m3, wconv)
 
     def forward(p, _):
         here = pl.ds(pl.multiple_of(p * span, span), span)
-        pre = jnp.zeros((span, C), F32)
-        for i in range(3):
-            pre = pre + dot(
-                m3[pl.ds(pl.multiple_of(p * span + i * CY, CY), span), :], wconv[i]
-            )
+        pre = conv[pl.ds(4 * p, 4)].reshape(span, C)
         occupied = jnp.concatenate([mask[p]] * 4, axis=0)
         sig = sigmoid(pre)
         feature = (occupied * (pre * sig)).astype(BF16)
@@ -332,18 +358,18 @@
         gp[here, :] = value.astype(BF16)
         return 0
 
-    lax.fori_loop(0, d.tx, forward, 0)
+    lax.fori_loop(0, d.tx, forward, 0, unroll=True)
     halo_start(1)
     maps_out = pltpu.make_async_copy(maps, maps_o, out_sem.at[0])
     maps_out.start()
 
-    def last(half, total, rows):
+    def last(total, rows):
         rows[pl.ds(0, d.rlp, stride=2), :] = total[:, 0:128]
         rows[pl.ds(1, d.rlp, stride=2), :] = total[:, 128:256]
-        for k in range(d.nb):
-            at = half * d.nb + k
+        for k in range(Y):
+            at = k
             ls[at] = rows[k * d.hb : k * d.hb + d.hbp, :].astype(BF16)
-            block = block_of(half, k)
+            block = first_block + k
             copy = rcopy(ls.at[at], l_r.at[my_y], l_send, l_recv, owner(block))
             local = pltpu.make_async_copy(ls.at[at], l_r.at[my_y], l_recv)
 
@@ -393,7 +419,8 @@
         hxs[k] = hs32[k * d.hx : (k + 1) * d.hx, :].astype(BF16)
     hx_wait = send_all(hxs, hx_r, X, s, x_peer, hx_send, hx_recv)
 
-    halo_finish(1, g3, False)
+    halo_inner(g3)
+    conv_inner(g3, wt)
 
     hx_wait.wait_recv()
     total = hs32[pl.ds(pl.multiple_of(s * d.hx, d.hx), d.hx), :]
@@ -408,18 +435,16 @@
 
     core_copy.wait_recv()
     cs32[...] = dw32[mine, :] + core_r[...].astype(F32)
-    for k in range(Z):
-        az[k] = cs32[k * d.az : k * d.az + d.azp, :].astype(BF16)
-    az_wait = send_all(az, az_r, Z, z, z_peer, az_send, az_recv)
     for k in range(X):
-        bx[k] = cs32[d.ra + k * d.bx : d.ra + (k + 1) * d.bx, :].astype(BF16)
+        bx[k] = cs32[k * d.bx : (k + 1) * d.bx, :].astype(BF16)
     bx_wait = send_all(bx, bx_r, X, s, x_peer, bx_send, bx_recv)
+
+    halo_finish(1, g3, False)
+    conv_edges(1, g3, wt)
 
     def backward(p, _):
         here = pl.ds(pl.multiple_of(p * span, span), span)
-        acc = jnp.zeros((span, C), F32)
-        for i in range(3):
-            acc = acc + dot(g3[pl.ds(pl.multiple_of(p * span + i * CY, CY), span), :], wt[i])
+        acc = conv[pl.ds(4 * p, 4)].reshape(span, C)
         acc = acc * jnp.concatenate([mask[p]] * 4, axis=0)
         gi[here, :] = acc.astype(BF16)
         m32[pl.ds(4 * p, 4)] = acc.reshape(4, CY, C)
@@ -428,7 +453,7 @@
             tiles[p * d.ty + q] = jnp.concatenate(parts, axis=0).astype(BF16)
         return 0
 
-    lax.fori_loop(0, d.tx, backward, 0)
+    lax.fori_loop(0, d.tx, backward, 0, unroll=True)
     gin_out = pltpu.make_async_copy(gi, gin_o, out_sem.at[1])
     gin_out.start()
 
@@ -453,8 +478,17 @@
     own_out = pltpu.make_async_copy(ret.at[me], gcam_o.at[me], out_sem.at[2])
     own_out.start()
 
+    hy_wait.wait_recv()
+    total = hy[...].astype(F32)
+    for k in range(Y - 1):
+        total = total + hy_r[k].astype(F32)
+    hpart[z] = total.astype(BF16)
+    part = hpart.at[z]
+    for k in range(1, Z):
+        rcopy(part, part, gz_send, gz_recv, z_peer(k)).start()
+
     bx_wait.wait_recv()
-    total = cs32[pl.ds(pl.multiple_of(d.ra + s * d.bx, 8), d.bx), :]
+    total = cs32[pl.ds(pl.multiple_of(s * d.bx, 8), d.bx), :]
     for k in range(X - 1):
         total = total + bx_r[k].astype(F32)
     bxsum[0 : d.bx, :] = total
@@ -463,26 +497,6 @@
         bz32[k] = part
         bz[k] = part.astype(BF16)
     bz_wait = send_all(bz, bz_r, Z, z, z_peer, bz_send, bz_recv)
-
-    hy_wait.wait_recv()
-    total = hy[...].astype(F32)
-    for k in range(Y - 1):
-        total = total + hy_r[k].astype(F32)
-    hpart[z] = total.astype(BF16)
-    part = hpart.at[z]
-    for k in range(1, Z):
-        rcopy(part, part, gz_send, gz_recv, z_peer(k)).start()
-
-    az_wait.wait_recv()
-    total = cs32[pl.ds(pl.multiple_of(z * d.az, 8), d.azp), :]
-    for k in range(Z - 1):
-        total = total + az_r[k].astype(F32)
-    azsum[0 : d.azp, :] = total
-    for k in range(X):
-        part = azsum[k * d.rl : k * d.rl + d.rlp, :]
-        ax32[k] = part
-        ax[k] = part.astype(BF16)
-    ax_wait = send_all(ax, ax_r, X, s, x_peer, ax_send, ax_recv)
 
     parts = hpart.at[pl.ds(0, Z - 1)]
     gz_wait = rcopy(parts, parts, gz_send, gz_recv, other_core)
@@ -498,13 +512,7 @@
     total = bz32[z]
     for k in range(Z - 1):
         total = total + bz_r[k].astype(F32)
-    last(1, total, bhrow)
-    ax_wait.wait_recv()
-    total = ax32[s]
-    for k in range(X - 1):
-        total = total + ax_r[k].astype(F32)
-    last(0, total, ahrow)
-
+    last(total, brow)
     parts = hall.at[core, pl.ds(0, X - 1)]
     gx_wait = rcopy(parts, parts, gx_send, gx_recv, other_core)
     gx_wait.wait_recv()
@@ -541,7 +549,7 @@
         rcopy(rows_s.at[k], rows_r.at[k], row_send.at[k], row_recv.at[k], other_core).wait_send()
         rcopy(cols_r.at[k], cols_r.at[k], col_send.at[k], col_recv.at[k], other_core).wait_send()
     for wait in (
-        az_wait, ax_wait, bx_wait, bz_wait, hx_wait, hz_wait, hy_wait, gz_wait, gx_wait,
+        bx_wait, bz_wait, hx_wait, hz_wait, hy_wait, gz_wait, gx_wait,
         core_copy, hcore_copy, gcore,
     ):
         wait.wait_send()
@@ -606,16 +614,15 @@
         b16(cells, outc), i32(d.tx, d.ty), i32(d.tx, d.ty), pltpu.SMEM((d.tx, d.ty), jnp.int32),
         i32(8, 128), pltpu.SMEM((8, 128), jnp.int32),
         b16(3, 3 * C, C), b16(head, C), b16(outc, head), f32(d.tx, cells_y, C),
-        f32(cells_x, cells_y, C), b16((cells_x + 2) * cells_y, 3 * C), b16((cells_x + 2) * cells_y, 3 * C),
+        f32(cells_x, cells_y, C), f32(cells_x, cells_y, C),
+        b16((cells_x + 2) * cells_y, 3 * C), b16((cells_x + 2) * cells_y, 3 * C),
         b16(2, 2, cells_y, C), b16(2, 2, cells_y, C),
         b16(2, 2, d.colp, C), b16(2, 2, 3, d.colp, C),
         b16(cells, C), b16(cells, head), b16(cells, head), b16(cells, outc), b16(cells, C),
         b16(cells, C), b16(d.tiles, 16, C), b16(N, 2, 16, C),
         f32(d.rows, C), b16(d.rows, C), b16(d.rc, C), f32(d.rc, C),
-        b16(Z, d.azp, C), b16(Z - 1, d.azp, C), f32(d.azp + d.rlp, C),
-        f32(X, d.rlp, C), b16(X, d.rlp, C), b16(X - 1, d.rlp, C), f32(2 * d.rlp, 128),
         b16(X, d.bx, C), b16(X - 1, d.bx, C), f32(d.bx + d.rlp, C),
-        f32(Z, d.rlp, C), b16(Z, d.rlp, C), b16(Z - 1, d.rlp, C), f32(2 * d.rlp, 128),
+        f32(Z, d.rlp, C), b16(Z, d.rlp, C), b16(Z - 1, d.rlp, C), f32(2 * d.rlp + 16, 128),
         b16(Y, d.hbp, 128), b16(Y, d.hbp, 128),
         f32(d.hrows, C), b16(d.hrows, C), b16(d.hc, C), f32(d.hc, C),
         b16(X, d.hx, C), b16(X - 1, d.hx, C), f32(d.hx + 16, C),
@@ -624,7 +631,7 @@
         b16(Z, d.hzp, C), f32(d.hx + 16, C), b16(2, X, d.hx, C),
         dma((9,)), dma((3,)),
         dma, dma, dma, dma, dma((2,)), dma((2,)), dma((2,)), dma((2,)), dma((3,)), dma((3,)),
-        *[dma] * 20,
+        *[dma] * 16,
     ]
     results = pl.pallas_call(
         functools.partial(kernel, d),

time: 80.2 us -> 76.6 us (0.955)
  the two profiles are of different devices: /device:TPU:1 before, /device:TPU:9 now
where the time goes in v3:
time: 76.6 us; the launch traced here: 76.5 us
  Pallas kernels  75.8 us (99%)
    pallas_call x1, Pallas kernels, per_device(): pl.pallas_call(functools.partial(kernel, d), out_shape=(jax.ShapeDtypeStr...  73.4 us
    pallas_call x1, Pallas kernels, per_device(): pl.pallas_call(copy_kernel, out_shape=tuple((jax.ShapeDtypeStruct(a.shape...  2.4 us

profile of v3, /device:TPU:9, one launch (start us, length us, event | category | flops | bytes accessed | tf_op | source)
XLA Modules:
  0.0 76.5 jit_solution(11520750918024622835)
XLA Ops:
  0.6 73.4 %shard_map.127 = (bf16[1024,128]{1,0:T(8,128)(2,1)}, bf16[1024,256]{1,0:T(8,128)(2,1)}, bf16[32,2,16,256]{3,2,1,0:T(8,128)(2,1)}, f32[9,128]{1,0:T(8,128)}, f32[256,512]{1,0:T(8,128)}, /*index=5*/f32[512,128]{1,0:T(8,128)}) custom-call(bf16[32,2,16,256]{3,2,1,0:T(8,128)(2,1)} %bitcast.11, bf16[1024,256]{1,0:T(8,128)(2,1)} %bitcast.12, s32[4,16]{1,0:T(4,128)} %bitcast.14, ...), custom_call_target="tpu_custom_call" | custom-call | tf_op jit(solution)/shard_map/pallas_call | solution.py:636
  74.1 2.4 %shard_map.128 = (bf16[1024,128]{1,0:T(8,128)(2,1)}, bf16[1024,256]{1,0:T(8,128)(2,1)}, bf16[32,2,16,256]{3,2,1,0:T(8,128)(2,1)}, f32[9,128]{1,0:T(8,128)}, f32[256,512]{1,0:T(8,128)}, /*index=5*/f32[512,128]{1,0:T(8,128)}) custom-call(bf16[1024,128]{1,0:T(8,128)(2,1)} %get-tuple-element.18.refs_0_, bf16[1024,256]{1,0:T(8,128)(2,1)} %get-tuple-element.19.refs_1_, ...), custom_call_target="tpu_custom_call" | custom-call | tf_op jit(solution)/shard_map/pallas_call | solution.py:662

commit v4 on v3

--- a/solution.py
+++ b/solution.py
@@ -11,6 +11,7 @@
 MESH = pl.DeviceIdType.MESH
 F32 = jnp.float32
 BF16 = jnp.bfloat16
+VMEM_BYTES = (62 * 1024 - 256) * 1024
 
 
 def pad16(rows):
@@ -73,7 +74,7 @@
     arrived, lidar, wconv, hup, hout, cot, act, tvec, tsrc, inv_v, inv,
     wt, hup_t, hout_t, mask,
     m32, conv, m3, g3, rows_s, rows_r, cols_s, cols_r,
-    feat, hid, gh, maps, gp, gi, tiles, ret,
+    feat, hid, gh, gp, tiles, ret,
     dw32, dwb, core_r, cs32,
     bx, bx_r, bxsum, bz32, bz, bz_r, brow, ls, l_r,
     h32, hb, hcore_r, hs32, hxs, hx_r, hxsum, hzs32, hzs, hz_r, hy, hy_r, hpart, hpack, hall,
@@ -350,7 +351,7 @@
         sig = sigmoid(up)
         hidden = (up * sig).astype(BF16)
         hid[here, :] = hidden
-        maps[here, :] = dot(hidden, hout[...]).astype(BF16)
+        maps_o[here, :] = dot(hidden, hout[...]).astype(BF16)
         grad = (dot(cot[here, :], hout_t[...]) * (sig * (1.0 + up * (1.0 - sig)))).astype(BF16)
         gh[here, :] = grad
         value = dot(grad, hup_t[...]) * m32[lines].reshape(span, C)
@@ -360,9 +361,6 @@
 
     lax.fori_loop(0, d.tx, forward, 0, unroll=True)
     halo_start(1)
-    maps_out = pltpu.make_async_copy(maps, maps_o, out_sem.at[0])
-    maps_out.start()
-
     def last(total, rows):
         rows[pl.ds(0, d.rlp, stride=2), :] = total[:, 0:128]
         rows[pl.ds(1, d.rlp, stride=2), :] = total[:, 128:256]
@@ -446,7 +444,7 @@
         here = pl.ds(pl.multiple_of(p * span, span), span)
         acc = conv[pl.ds(4 * p, 4)].reshape(span, C)
         acc = acc * jnp.concatenate([mask[p]] * 4, axis=0)
-        gi[here, :] = acc.astype(BF16)
+        gin_o[here, :] = acc.astype(BF16)
         m32[pl.ds(4 * p, 4)] = acc.reshape(4, CY, C)
         for q in range(d.ty):
             parts = [m32[4 * p + dx, 4 * q : 4 * q + 4, :] for dx in range(4)]
@@ -454,9 +452,6 @@
         return 0
 
     lax.fori_loop(0, d.tx, backward, 0, unroll=True)
-    gin_out = pltpu.make_async_copy(gi, gin_o, out_sem.at[1])
-    gin_out.start()
-
     hz_wait.wait_recv()
     total = hzs32[z]
     for k in range(Z - 1):
@@ -475,7 +470,7 @@
     each_peer(b_start)
     for slot in range(2):
         ret[me, slot] = tiles[inv[0, me * 2 + slot]]
-    own_out = pltpu.make_async_copy(ret.at[me], gcam_o.at[me], out_sem.at[2])
+    own_out = pltpu.make_async_copy(ret.at[me], gcam_o.at[me], out_sem)
     own_out.start()
 
     hy_wait.wait_recv()
@@ -563,22 +558,14 @@
     def _():
         rcopy(ls, ls, l_send, l_recv, other_core).wait_send()
 
-    maps_out.wait()
-    gin_out.wait()
     own_out.wait()
 
 
 def copy_kernel(*refs):
-    loads = [
-        pltpu.make_async_copy(refs[k], refs[12 + k], refs[18].at[k]) for k in range(6)
+    stores = [
+        pltpu.make_async_copy(refs[k], refs[6 + k], refs[12].at[k]) for k in range(6)
     ]
-    stores = [
-        pltpu.make_async_copy(refs[12 + k], refs[6 + k], refs[18].at[k]) for k in range(6)
-    ]
-    for load in loads:
-        load.start()
-    for load, store in zip(loads, stores):
-        load.wait()
+    for store in stores:
         store.start()
     for store in stores:
         store.wait()
@@ -618,8 +605,8 @@
         b16((cells_x + 2) * cells_y, 3 * C), b16((cells_x + 2) * cells_y, 3 * C),
         b16(2, 2, cells_y, C), b16(2, 2, cells_y, C),
         b16(2, 2, d.colp, C), b16(2, 2, 3, d.colp, C),
-        b16(cells, C), b16(cells, head), b16(cells, head), b16(cells, outc), b16(cells, C),
-        b16(cells, C), b16(d.tiles, 16, C), b16(N, 2, 16, C),
+        b16(cells, C), b16(cells, head), b16(cells, head), b16(cells, C),
+        b16(d.tiles, 16, C), b16(N, 2, 16, C),
         f32(d.rows, C), b16(d.rows, C), b16(d.rc, C), f32(d.rc, C),
         b16(X, d.bx, C), b16(X - 1, d.bx, C), f32(d.bx + d.rlp, C),
         f32(Z, d.rlp, C), b16(Z, d.rlp, C), b16(Z - 1, d.rlp, C), f32(2 * d.rlp + 16, 128),
@@ -629,25 +616,25 @@
         f32(Z, d.hzp, C), b16(Z, d.hzp, C), b16(Z - 1, d.hzp, C),
         b16(d.hzp, C), b16(Y - 1, d.hzp, C),
         b16(Z, d.hzp, C), f32(d.hx + 16, C), b16(2, X, d.hx, C),
-        dma((9,)), dma((3,)),
+        dma((9,)), dma,
         dma, dma, dma, dma, dma((2,)), dma((2,)), dma((2,)), dma((2,)), dma((3,)), dma((3,)),
         *[dma] * 16,
     ]
     results = pl.pallas_call(
         functools.partial(kernel, d),
         out_shape=(
-            jax.ShapeDtypeStruct((cells, outc), BF16),
-            jax.ShapeDtypeStruct((cells, C), BF16),
-            jax.ShapeDtypeStruct((N, 2, 16, C), BF16),
-            jax.ShapeDtypeStruct((d.hb, 128), F32),
-            jax.ShapeDtypeStruct((C, head), F32),
-            jax.ShapeDtypeStruct((head, outc), F32),
+            pltpu.VMEM((cells, outc), BF16),
+            pltpu.VMEM((cells, C), BF16),
+            pltpu.VMEM((N, 2, 16, C), BF16),
+            pltpu.VMEM((d.hb, 128), F32),
+            pltpu.VMEM((C, head), F32),
+            pltpu.VMEM((head, outc), F32),
         ),
         in_specs=[anyw] * 8,
-        out_specs=(anyw, anyw, anyw, vmem, vmem, vmem),
+        out_specs=(vmem,) * 6,
         scratch_shapes=scratch,
         compiler_params=pltpu.CompilerParams(
-            collective_id=0, has_side_effects=True, vmem_limit_bytes=64 * 1024 * 1024
+            collective_id=0, has_side_effects=True, vmem_limit_bytes=VMEM_BYTES
         ),
     )(
         cam_send.reshape(N, 2, 16, C),
@@ -662,10 +649,10 @@
     maps, gin, gcam, gconv, gup, gout = pl.pallas_call(
         copy_kernel,
         out_shape=tuple(jax.ShapeDtypeStruct(a.shape, a.dtype) for a in results),
-        in_specs=[anyw] * 6,
+        in_specs=[vmem] * 6,
         out_specs=(anyw,) * 6,
-        scratch_shapes=[*[pltpu.VMEM(a.shape, a.dtype) for a in results], dma((6,))],
-        compiler_params=pltpu.CompilerParams(vmem_limit_bytes=64 * 1024 * 1024),
+        scratch_shapes=[dma((6,))],
+        compiler_params=pltpu.CompilerParams(vmem_limit_bytes=1024 * 1024),
     )(*results)
     return (
         maps.reshape(1, cells_x, cells_y, outc),

time: 76.6 us -> 74.4 us (0.971)
  the two profiles are of different devices: /device:TPU:9 before, /device:TPU:8 now
where the time goes in v4:
time: 74.4 us; the launch traced here: 74.3 us
  Pallas kernels  73.7 us (99%)
    pallas_call x1, Pallas kernels, per_device(): pl.pallas_call(functools.partial(kernel, d), out_shape=(pltpu.VMEM((cells...  72.3 us

profile of v4, /device:TPU:8, one launch (start us, length us, event | category | flops | bytes accessed | tf_op | source)
XLA Modules:
  0.0 74.3 jit_solution(15235554285348243471)
XLA Ops:
  0.6 72.3 %shard_map.127 = (bf16[1024,128]{1,0:T(8,128)(2,1)S(1)}, bf16[1024,256]{1,0:T(8,128)(2,1)S(1)}, bf16[32,2,16,256]{3,2,1,0:T(8,128)(2,1)S(1)}, f32[9,128]{1,0:T(8...) custom-call(bf16[32,2,16,256]{3,2,1,0:T(8,128)(2,1)} %bitcast.11, bf16[1024,256]{1,0:T(8,128)(2,1)} %bitcast.12, ...), custom_call_target="tpu_custom_call" | custom-call | tf_op jit(solution)/shard_map/pallas_call | solution.py:623
  72.9 1.4 %shard_map.128 = (bf16[1024,128]{1,0:T(8,128)(2,1)}, bf16[1024,256]{1,0:T(8,128)(2,1)}, bf16[32,2,16,256]{3,2,1,0:T(8,128)(2,1)}, f32[9,128]{1,0:T(8,128)}, f32[256,512]{1,0:T(8,128)}, /*index=5*/f32[512,128]{1,0:T(8,128)}) custom-call(bf16[1024,128]{1,0:T(8,128)(2,1)S(1)} %get-tuple-element.18.refs_0_, bf16[1024,256]{1,0:T(8,128)(2,1)S(1)} %get-tuple-element.19.refs_1_, ...), custom_call_target="tpu_custom_call" | custom-call | tf_op jit(solution)/shard_map/pallas_call | solution.py:649

commit v5 on v4

--- a/solution.py
+++ b/solution.py
@@ -54,6 +54,10 @@
         self.colp = pad16(cells_x)
         self.rows = 9 * channels
         self.rc = self.rows // 2
+        self.units = n_src * self.YL
+        self.u = self.rc // self.units
+        self.up = pad16(self.u)
+        self.uz = self.u // self.Z
         self.bx = self.rc // self.X
         self.rl = self.bx // self.Z
         self.rlp = pad16(self.rl)
@@ -76,7 +80,7 @@
     m32, conv, m3, g3, rows_s, rows_r, cols_s, cols_r,
     feat, hid, gh, gp, tiles, ret,
     dw32, dwb, core_r, cs32,
-    bx, bx_r, bxsum, bz32, bz, bz_r, brow, ls, l_r,
+    bx, bx_r, bxsum, bz32, bz, bz_r, brow, l32, ls, l_r,
     h32, hb, hcore_r, hs32, hxs, hx_r, hxsum, hzs32, hzs, hz_r, hy, hy_r, hpart, hpack, hall,
     in_sem, out_sem,
     a_send, a_recv, b_send, b_recv, row_send, row_recv, col_send, col_recv, core_send, core_recv,
@@ -134,21 +138,7 @@
 
     other_core = (s, yl * 2 + 1 - core, r)
 
-    my_block = (s * d.GX + g) * d.GY + r
-    group = my_block // Y
-    from_core, from_x, from_z = group // (X * Z), (group // Z) % X, group % Z
     my_y = yl * 2 + yh
-    first_block = ((core * X + s) * Z + z) * Y
-
-    def owner(block):
-        return (block // (d.GX * d.GY), (block // d.GY) % d.GX, block % d.GY)
-
-    def last_sender(at):
-        return (from_x, (at // 2) * 2 + from_core, from_z * 2 + at % 2)
-
-    self_group = jnp.logical_and(
-        jnp.logical_and(from_core == core, from_z == z), from_x == s
-    )
 
     barrier = pltpu.get_barrier_semaphore()
 
@@ -167,14 +157,6 @@
         for near in (-1, 0, 1):
             greet((s, (g + near + d.GX) % d.GX, (r + side + d.GY) % d.GY))
             count += 1
-    for at in range(Y):
-        is_self = jnp.logical_and(self_group, my_y == at)
-
-        @pl.when(jnp.logical_not(is_self))
-        def _():
-            greet(last_sender(at))
-
-    count = count + Y - jnp.where(self_group, 1, 0)
     pl.semaphore_wait(barrier, count)
 
     def a_start(far, step):
@@ -361,24 +343,6 @@
 
     lax.fori_loop(0, d.tx, forward, 0, unroll=True)
     halo_start(1)
-    def last(total, rows):
-        rows[pl.ds(0, d.rlp, stride=2), :] = total[:, 0:128]
-        rows[pl.ds(1, d.rlp, stride=2), :] = total[:, 128:256]
-        for k in range(Y):
-            at = k
-            ls[at] = rows[k * d.hb : k * d.hb + d.hbp, :].astype(BF16)
-            block = first_block + k
-            copy = rcopy(ls.at[at], l_r.at[my_y], l_send, l_recv, owner(block))
-            local = pltpu.make_async_copy(ls.at[at], l_r.at[my_y], l_recv)
-
-            @pl.when(block != my_block)
-            def _():
-                copy.start()
-
-            @pl.when(block == my_block)
-            def _():
-                local.start()
-
     term = dot_tn(feat[...], gh[...])
     for half in range(d.head // C):
         h32[half * C : (half + 1) * C, :] = term[:, half * C : (half + 1) * C]
@@ -402,13 +366,13 @@
             )
             at = pl.ds(pl.multiple_of(i * (3 * C) + j * C, C), C)
             dw32[at, :] = term
-            dwb[at, :] = term.astype(BF16)
         return 0
 
     lax.fori_loop(0, 3, tap_grads, 0)
-    mine = pl.ds(pl.multiple_of(core * d.rc, d.rc), d.rc)
-    theirs = pl.ds(pl.multiple_of((1 - core) * d.rc, d.rc), d.rc)
-    core_copy = rcopy(dwb.at[theirs], core_r, core_send.at[0], core_recv.at[0], other_core)
+    for k in range(d.units):
+        theirs = pl.ds(pl.multiple_of((2 * k + 1 - core) * d.u, 8), d.u)
+        dwb[k, 0 : d.u, :] = dw32[theirs, :].astype(BF16)
+    core_copy = rcopy(dwb, core_r, core_send.at[0], core_recv.at[0], other_core)
     core_copy.start()
 
     hcore_copy.wait_recv()
@@ -432,7 +396,9 @@
     hz_wait = send_all(hzs, hz_r, Z, z, z_peer, hz_send, hz_recv)
 
     core_copy.wait_recv()
-    cs32[...] = dw32[mine, :] + core_r[...].astype(F32)
+    for k in range(d.units):
+        mine = pl.ds(pl.multiple_of((2 * k + core) * d.u, 8), d.u)
+        cs32[k * d.u : (k + 1) * d.u, :] = dw32[mine, :] + core_r[k, 0 : d.u, :].astype(F32)
     for k in range(X):
         bx[k] = cs32[k * d.bx : (k + 1) * d.bx, :].astype(BF16)
     bx_wait = send_all(bx, bx_r, X, s, x_peer, bx_send, bx_recv)
@@ -488,9 +454,10 @@
         total = total + bx_r[k].astype(F32)
     bxsum[0 : d.bx, :] = total
     for k in range(Z):
-        part = bxsum[k * d.rl : k * d.rl + d.rlp, :]
-        bz32[k] = part
-        bz[k] = part.astype(BF16)
+        for y in range(d.YL):
+            here = y * d.u + k * d.uz
+            bz32[k, y * d.uz : (y + 1) * d.uz, :] = bxsum[here : here + d.uz, :]
+        bz[k] = bz32[k].astype(BF16)
     bz_wait = send_all(bz, bz_r, Z, z, z_peer, bz_send, bz_recv)
 
     parts = hpart.at[pl.ds(0, Z - 1)]
@@ -507,16 +474,23 @@
     total = bz32[z]
     for k in range(Z - 1):
         total = total + bz_r[k].astype(F32)
-    last(total, brow)
+    brow[pl.ds(0, d.rlp, stride=2), :] = total[:, 0:128]
+    brow[pl.ds(1, d.rlp, stride=2), :] = total[:, 128:256]
+    for k in range(Y):
+        part = brow[k * d.hb : k * d.hb + d.hbp, :]
+        l32[k] = part
+        ls[k] = part.astype(BF16)
+    l_wait = send_all(ls, l_r, Y, my_y, y_peer, l_send, l_recv)
+
     parts = hall.at[core, pl.ds(0, X - 1)]
     gx_wait = rcopy(parts, parts, gx_send, gx_recv, other_core)
     gx_wait.wait_recv()
     gcore = rcopy(hall.at[core], hall.at[core], core_send.at[2], core_recv.at[2], other_core)
     gcore.start()
 
-    total = jnp.zeros((d.hbp, 128), F32)
-    pltpu.make_async_copy(ls, l_r, l_recv).wait()
-    for k in range(Y):
+    l_wait.wait_recv()
+    total = l32[my_y]
+    for k in range(Y - 1):
         total = total + l_r[k].astype(F32)
     gconv_o[...] = total[0 : d.hb, :] * d.scale
 
@@ -545,18 +519,9 @@
         rcopy(cols_r.at[k], cols_r.at[k], col_send.at[k], col_recv.at[k], other_core).wait_send()
     for wait in (
         bx_wait, bz_wait, hx_wait, hz_wait, hy_wait, gz_wait, gx_wait,
-        core_copy, hcore_copy, gcore,
+        l_wait, core_copy, hcore_copy, gcore,
     ):
         wait.wait_send()
-
-    @pl.when(self_group)
-    def _():
-        parts = ls.at[pl.ds(0, Y - 1)]
-        rcopy(parts, parts, l_send, l_recv, other_core).wait_send()
-
-    @pl.when(jnp.logical_not(self_group))
-    def _():
-        rcopy(ls, ls, l_send, l_recv, other_core).wait_send()
 
     own_out.wait()
 
@@ -607,10 +572,10 @@
         b16(2, 2, d.colp, C), b16(2, 2, 3, d.colp, C),
         b16(cells, C), b16(cells, head), b16(cells, head), b16(cells, C),
         b16(d.tiles, 16, C), b16(N, 2, 16, C),
-        f32(d.rows, C), b16(d.rows, C), b16(d.rc, C), f32(d.rc, C),
+        f32(d.rows, C), b16(d.units, d.up, C), b16(d.units, d.up, C), f32(d.rc, C),
         b16(X, d.bx, C), b16(X - 1, d.bx, C), f32(d.bx + d.rlp, C),
         f32(Z, d.rlp, C), b16(Z, d.rlp, C), b16(Z - 1, d.rlp, C), f32(2 * d.rlp + 16, 128),
-        b16(Y, d.hbp, 128), b16(Y, d.hbp, 128),
+        f32(Y, d.hbp, 128), b16(Y, d.hbp, 128), b16(Y - 1, d.hbp, 128),
         f32(d.hrows, C), b16(d.hrows, C), b16(d.hc, C), f32(d.hc, C),
         b16(X, d.hx, C), b16(X - 1, d.hx, C), f32(d.hx + 16, C),
         f32(Z, d.hzp, C), b16(Z, d.hzp, C), b16(Z - 1, d.hzp, C),

time: 74.4 us -> 71 us (0.954)
  the two profiles are of different devices: /device:TPU:8 before, /device:TPU:1 now
where the time goes in v5:
time: 71 us; the launch traced here: 70.9 us
  Pallas kernels  70.2 us (99%)
    pallas_call x1, Pallas kernels, per_device(): pl.pallas_call(functools.partial(kernel, d), out_shape=(pltpu.VMEM((cells...  68.9 us

profile of v5, /device:TPU:1, one launch (start us, length us, event | category | flops | bytes accessed | tf_op | source)
XLA Modules:
  0.0 70.9 jit_solution(11113429593806137618)
XLA Ops:
  0.6 68.9 %shard_map.127 = (bf16[1024,128]{1,0:T(8,128)(2,1)S(1)}, bf16[1024,256]{1,0:T(8,128)(2,1)S(1)}, bf16[32,2,16,256]{3,2,1,0:T(8,128)(2,1)S(1)}, f32[9,128]{1,0:T(8...) custom-call(bf16[32,2,16,256]{3,2,1,0:T(8,128)(2,1)} %bitcast.11, bf16[1024,256]{1,0:T(8,128)(2,1)} %bitcast.12, ...), custom_call_target="tpu_custom_call" | custom-call | tf_op jit(solution)/shard_map/pallas_call | solution.py:588
  69.5 1.4 %shard_map.128 = (bf16[1024,128]{1,0:T(8,128)(2,1)}, bf16[1024,256]{1,0:T(8,128)(2,1)}, bf16[32,2,16,256]{3,2,1,0:T(8,128)(2,1)}, f32[9,128]{1,0:T(8,128)}, f32[256,512]{1,0:T(8,128)}, /*index=5*/f32[512,128]{1,0:T(8,128)}) custom-call(bf16[1024,128]{1,0:T(8,128)(2,1)S(1)} %get-tuple-element.18.refs_0_, bf16[1024,256]{1,0:T(8,128)(2,1)S(1)} %get-tuple-element.19.refs_1_, ...), custom_call_target="tpu_custom_call" | custom-call | tf_op jit(solution)/shard_map/pallas_call | solution.py:614

commit v6 on v5

--- a/solution.py
+++ b/solution.py
@@ -433,7 +433,10 @@
             ret[to, slot] = tiles[inv[0, to * 2 + slot]]
         rcopy(ret.at[to], gcam_o.at[me], b_send, b_recv, device).start()
 
-    each_peer(b_start)
+    for step in range(2):
+        for far in order:
+            if far or step:
+                b_start(far, step)
     for slot in range(2):
         ret[me, slot] = tiles[inv[0, me * 2 + slot]]
     own_out = pltpu.make_async_copy(ret.at[me], gcam_o.at[me], out_sem)
@@ -460,15 +463,25 @@
         bz[k] = bz32[k].astype(BF16)
     bz_wait = send_all(bz, bz_r, Z, z, z_peer, bz_send, bz_recv)
 
+    def b_rest(step, _):
+        for far in order:
+            b_start(far, step)
+        return 0
+
+    lax.fori_loop(2, 2 * X, b_rest, 0)
+
     parts = hpart.at[pl.ds(0, Z - 1)]
     gz_wait = rcopy(parts, parts, gz_send, gz_recv, other_core)
     gz_wait.wait_recv()
     for k in range(Z):
         hpack[k * d.hz : k * d.hz + d.hzp, :] = hpart[k].astype(F32)
-    hall[core, s] = hpack[0 : d.hx, :].astype(BF16)
-    part = hall.at[core, s]
+    hall[core * X + s] = hpack[0 : d.hx, :].astype(BF16)
+    part = hall.at[core * X + s]
     for k in range(1, X):
         rcopy(part, part, gx_send, gx_recv, x_peer(k)).start()
+    for k in range(X):
+        across = ((s + k) % X, yl * 2 + 1 - core, r)
+        rcopy(part, part, gx_send, gx_recv, across).start()
 
     bz_wait.wait_recv()
     total = bz32[z]
@@ -482,11 +495,8 @@
         ls[k] = part.astype(BF16)
     l_wait = send_all(ls, l_r, Y, my_y, y_peer, l_send, l_recv)
 
-    parts = hall.at[core, pl.ds(0, X - 1)]
+    parts = hall.at[pl.ds(0, 2 * X - 1)]
     gx_wait = rcopy(parts, parts, gx_send, gx_recv, other_core)
-    gx_wait.wait_recv()
-    gcore = rcopy(hall.at[core], hall.at[core], core_send.at[2], core_recv.at[2], other_core)
-    gcore.start()
 
     l_wait.wait_recv()
     total = l32[my_y]
@@ -494,13 +504,11 @@
         total = total + l_r[k].astype(F32)
     gconv_o[...] = total[0 : d.hb, :] * d.scale
 
-    rcopy(
-        hall.at[1 - core], hall.at[1 - core], core_send.at[2], core_recv.at[2], other_core
-    ).wait_recv()
+    gx_wait.wait_recv()
     for c in range(2):
         for x in range(X):
             at = c * d.hc + x * d.hx
-            h32[at : at + d.hx, :] = hall[c, x].astype(F32)
+            h32[at : at + d.hx, :] = hall[c * X + x].astype(F32)
     for half in range(d.head // C):
         gup_o[:, half * C : (half + 1) * C] = h32[half * C : (half + 1) * C, :] * d.scale
     for half in range(2):
@@ -519,7 +527,7 @@
         rcopy(cols_r.at[k], cols_r.at[k], col_send.at[k], col_recv.at[k], other_core).wait_send()
     for wait in (
         bx_wait, bz_wait, hx_wait, hz_wait, hy_wait, gz_wait, gx_wait,
-        l_wait, core_copy, hcore_copy, gcore,
+        l_wait, core_copy, hcore_copy,
     ):
         wait.wait_send()
 
@@ -580,9 +588,9 @@
         b16(X, d.hx, C), b16(X - 1, d.hx, C), f32(d.hx + 16, C),
         f32(Z, d.hzp, C), b16(Z, d.hzp, C), b16(Z - 1, d.hzp, C),
         b16(d.hzp, C), b16(Y - 1, d.hzp, C),
-        b16(Z, d.hzp, C), f32(d.hx + 16, C), b16(2, X, d.hx, C),
+        b16(Z, d.hzp, C), f32(d.hx + 16, C), b16(2 * X, d.hx, C),
         dma((9,)), dma,
-        dma, dma, dma, dma, dma((2,)), dma((2,)), dma((2,)), dma((2,)), dma((3,)), dma((3,)),
+        dma, dma, dma, dma, dma((2,)), dma((2,)), dma((2,)), dma((2,)), dma((2,)), dma((2,)),
         *[dma] * 16,
     ]
     results = pl.pallas_call(

time: 71 us -> 70.9 us (level)
  no operation moved by 1% of the time
where the time goes in v6:
time: 70.9 us; the launch traced here: 70.2 us
  Pallas kernels  69.6 us (98%)
    pallas_call x1, Pallas kernels, per_device(): pl.pallas_call(functools.partial(kernel, d), out_shape=(pltpu.VMEM((cells...  68.2 us

profile of v6, /device:TPU:1, one launch (start us, length us, event | category | flops | bytes accessed | tf_op | source)
XLA Modules:
  0.0 70.2 jit_solution(8152581961976087216)
XLA Ops:
  0.6 68.2 %shard_map.127 = (bf16[1024,128]{1,0:T(8,128)(2,1)S(1)}, bf16[1024,256]{1,0:T(8,128)(2,1)S(1)}, bf16[32,2,16,256]{3,2,1,0:T(8,128)(2,1)S(1)}, f32[9,128]{1,0:T(8...) custom-call(bf16[32,2,16,256]{3,2,1,0:T(8,128)(2,1)} %bitcast.11, bf16[1024,256]{1,0:T(8,128)(2,1)} %bitcast.12, ...), custom_call_target="tpu_custom_call" | custom-call | tf_op jit(solution)/shard_map/pallas_call | solution.py:596
  68.9 1.4 %shard_map.128 = (bf16[1024,128]{1,0:T(8,128)(2,1)}, bf16[1024,256]{1,0:T(8,128)(2,1)}, bf16[32,2,16,256]{3,2,1,0:T(8,128)(2,1)}, f32[9,128]{1,0:T(8,128)}, f32[256,512]{1,0:T(8,128)}, /*index=5*/f32[512,128]{1,0:T(8,128)}) custom-call(bf16[1024,128]{1,0:T(8,128)(2,1)S(1)} %get-tuple-element.18.refs_0_, bf16[1024,256]{1,0:T(8,128)(2,1)S(1)} %get-tuple-element.19.refs_1_, ...), custom_call_target="tpu_custom_call" | custom-call | tf_op jit(solution)/shard_map/pallas_call | solution.py:622
